TPU v7x, 32 devices: a whole 2x2x4 slice. The times are simulated.
32 devices in a mesh: patch: 8 (over z, y), rep: 4 (over x, core).
Axes of the slice: x: 2, y: 2, z: 4, core: 2. Of those that a mesh axis runs over, the one named last changes fastest.
Arguments:
- previous_state: float32 [4, 84, 24576], P('rep', None, 'patch'), may hold values from -6 to 6
- target_state: float32 [4, 84, 24576], P('rep', None, 'patch'), may hold values from -6 to 6
- noise_draws: float32 [4, 2, 84, 24576], P('rep', None, None, 'patch'), may hold values from -6 to 6
- noise_level: float32 [4, 2], P('rep'), may hold values from 0.3 to 3
- pixel_owner: int32 [4, 24576], P('rep', 'patch'), may hold values from 0 to 511, as said below
- mesh_to_grid: int32 [4, 3, 24576], P('rep', None, 'patch'), may hold values from 0 to 511, as said below
- neighbours: int32 [4, 4096, 16], P('rep', 'patch'), may hold values from 0 to 639, as said below
- halo_send: int32 [4, 1024], P('rep', 'patch'), may hold values from 0 to 511, as said below
- node_count: int32 [4, 8], P('rep', 'patch'), may hold values from 106 to 512, as said below
- pixel_count: int32 [4, 8], P('rep', 'patch'), may hold values from 640 to 3072, as said below
- w_encode: float32 [168, 512], P(None, ('patch', 'rep')), may hold values from -0.5 to 0.5
- w_project: float32 [512, 1536], P(('patch', 'rep')), may hold values from -0.25 to 0.25
- w_output: float32 [512, 512], P(('patch', 'rep')), may hold values from -0.5 to 0.5
- w_up: float32 [512, 2048], P(('patch', 'rep')), may hold values from -0.25 to 0.25
- w_down: float32 [2048, 512], P(('patch', 'rep')), may hold values from -0.125 to 0.125
- w_noise: float32 [32, 2048], P(None, ('patch', 'rep')), may hold values from -1 to 1
- w_decode: float32 [512, 84], P(('patch', 'rep')), may hold values from -0.25 to 0.25
- m_encode: float32 [168, 512], P(None, ('patch', 'rep')), may hold values from -0.00036621094 to 0.00036621094
- m_project: float32 [512, 1536], P(('patch', 'rep')), may hold values from -0.00036621094 to 0.00036621094
- m_output: float32 [512, 512], P(('patch', 'rep')), may hold values from -0.00036621094 to 0.00036621094
- m_up: float32 [512, 2048], P(('patch', 'rep')), may hold values from -0.00036621094 to 0.00036621094
- m_down: float32 [2048, 512], P(('patch', 'rep')), may hold values from -0.00036621094 to 0.00036621094
- m_noise: float32 [32, 2048], P(None, ('patch', 'rep')), may hold values from -0.00036621094 to 0.00036621094
- m_decode: float32 [512, 84], P(('patch', 'rep')), may hold values from -0.00036621094 to 0.00036621094
- v_encode: float32 [168, 512], P(None, ('patch', 'rep')), may hold values from 1.5747146e-08 to 6.286883e-08
- v_project: float32 [512, 1536], P(('patch', 'rep')), may hold values from 1.5747146e-08 to 6.286883e-08
- v_output: float32 [512, 512], P(('patch', 'rep')), may hold values from 1.5747146e-08 to 6.286883e-08
- v_up: float32 [512, 2048], P(('patch', 'rep')), may hold values from 1.5747146e-08 to 6.286883e-08
- v_down: float32 [2048, 512], P(('patch', 'rep')), may hold values from 1.5747146e-08 to 6.286883e-08
- v_noise: float32 [32, 2048], P(None, ('patch', 'rep')), may hold values from 1.5747146e-08 to 6.286883e-08
- v_decode: float32 [512, 84], P(('patch', 'rep')), may hold values from 1.5747146e-08 to 6.286883e-08
Outputs:
- new_encode: float32 [168, 512], P(None, ('patch', 'rep'))
- new_project: float32 [512, 1536], P(('patch', 'rep'))
- new_output: float32 [512, 512], P(('patch', 'rep'))
- new_up: float32 [512, 2048], P(('patch', 'rep'))
- new_down: float32 [2048, 512], P(('patch', 'rep'))
- new_noise: float32 [32, 2048], P(None, ('patch', 'rep'))
- new_decode: float32 [512, 84], P(('patch', 'rep'))
- moment_encode: float32 [168, 512], P(None, ('patch', 'rep'))
- moment_project: float32 [512, 1536], P(('patch', 'rep'))
- moment_output: float32 [512, 512], P(('patch', 'rep'))
- moment_up: float32 [512, 2048], P(('patch', 'rep'))
- moment_down: float32 [2048, 512], P(('patch', 'rep'))
- moment_noise: float32 [32, 2048], P(None, ('patch', 'rep'))
- moment_decode: float32 [512, 84], P(('patch', 'rep'))
- second_encode: float32 [168, 512], P(None, ('patch', 'rep'))
- second_project: float32 [512, 1536], P(('patch', 'rep'))
- second_output: float32 [512, 512], P(('patch', 'rep'))
- second_up: float32 [512, 2048], P(('patch', 'rep'))
- second_down: float32 [2048, 512], P(('patch', 'rep'))
- second_noise: float32 [32, 2048], P(None, ('patch', 'rep'))
- second_decode: float32 [512, 84], P(('patch', 'rep'))
- loss_sum: float32 [], replicated
- count_total: float32 [], replicated
- grad_norm: float32 [], replicated
Inputs may be any that keep to these rules, and one draw needn't show every extreme that they name: `pixel_owner`: names only live nodes of the pixel's patch. `mesh_to_grid`: names only live nodes of the pixel's patch. `neighbours`: entry 0 of each node's list is the node itself; entries of 512 or more name halo rows (lower patch's first). `halo_send`: only live nodes of the sending patch are named. `node_count`: the last patch of every sample is full. `pixel_count`: the last patch of every sample is full.
All inputs are finite; a program needn't handle non-finite values.
Results may differ from a plain program's by a relative error of at most 0.011.
Values may be sent and summed in bfloat16 or wider, within the bound.
A program may use at most 256 MiB of HBM per device.

v0:
```python
import jax
import jax.numpy as jnp
from jax import lax
from jax.sharding import PartitionSpec as P

HEADS = 4
HD = 128
FOUR = 32
NEIGH = 16
STEP = 5


LEARN_RATE = 0.03
BETA_ONE = 0.9
BETA_TWO = 0.95
EPSILON = 1e-08
DECAY_RATE = 0.1
THRESHOLD = 1.0


def padded(shard, sides, width):
    for axis, dim in sides:
        devices, length = (lax.axis_size(axis), shard.shape[dim])
        up = [(i, (i + 1) % devices) for i in range(devices)]
        down = [(j, i) for i, j in up]
        last = lax.slice_in_dim(shard, length - width, length, axis=dim)
        first = lax.slice_in_dim(shard, 0, width, axis=dim)
        before = lax.ppermute(last, axis, up)
        after = lax.ppermute(first, axis, down)
        shard = jnp.concatenate([before, shard, after], axis=dim)
    return shard


def fourier(level):
    frequency = 0.25 * (jnp.arange(FOUR // 2).astype(jnp.float32) + 1.0)
    angles = jnp.log(level) * frequency
    return jnp.concatenate([jnp.sin(angles), jnp.cos(angles)])


def adanorm(hidden, scaling, offset):
    centre = hidden - jnp.mean(hidden, axis=-1, keepdims=True)
    spread = jnp.mean(centre * centre, axis=-1, keepdims=True)
    return centre * lax.rsqrt(spread + 1e-05) * (1.0 + scaling) + offset


def split_near(extended, near_idx, model_width):
    node_rows = near_idx.shape[0]
    near = extended[near_idx]
    key_rows = near[:, :, :model_width].reshape(node_rows, NEIGH, HEADS, HD)
    val_rows = near[:, :, model_width:].reshape(node_rows, NEIGH, HEADS, HD)
    return (key_rows, val_rows)


def forward(
    gathered, noisy_in, level, previous, owner_hot, counted, decode_idx, near_idx, valid, send_idx
):
    w_encode, w_project, w_output, w_up, w_down, w_noise, w_decode = gathered
    model_width = w_project.shape[0]
    halo_rows = send_idx.shape[0] // 2
    c_in = lax.rsqrt(level * level + 1.0)
    c_skip = 1.0 / (level * level + 1.0)
    c_out = level * c_in
    inputs = jnp.concatenate([previous, noisy_in * c_in], axis=0).astype(jnp.bfloat16)
    encoded = jnp.einsum("cp,cd->pd", inputs, w_encode, preferred_element_type=jnp.float32).astype(
        jnp.bfloat16
    )
    summed = jnp.dot(owner_hot, encoded, preferred_element_type=jnp.float32)
    start_rows = summed / counted[:, None]
    waves = fourier(level)
    modulate = jnp.dot(
        waves[None, :], w_noise.astype(jnp.float32), precision=lax.Precision.HIGHEST
    )[0]
    normed = adanorm(
        start_rows, modulate[:model_width], modulate[model_width : 2 * model_width]
    ).astype(jnp.bfloat16)
    project = jnp.dot(normed, w_project, preferred_element_type=jnp.float32).astype(jnp.bfloat16)
    keyval = project[:, model_width:]
    arrived = padded(keyval[send_idx], (("patch", 0),), halo_rows)
    extended = jnp.concatenate([keyval, arrived[:halo_rows], arrived[3 * halo_rows :]], axis=0)
    queries = project[:, :model_width].reshape(-1, HEADS, HD)
    key_rows, val_rows = split_near(extended, near_idx, model_width)
    raw_scores = jnp.einsum("nhd,njhd->nhj", queries, key_rows, preferred_element_type=jnp.float32)
    scores = jnp.where(valid[:, None, :], raw_scores * HD ** (-0.5), -1e30)
    attention = jax.nn.softmax(scores, axis=-1)
    mixed_out = jnp.einsum(
        "nhj,njhd->nhd",
        attention.astype(jnp.bfloat16),
        val_rows,
        preferred_element_type=jnp.float32,
    )
    mixed_out = mixed_out.astype(jnp.bfloat16).reshape(-1, model_width)
    middle = start_rows + jnp.dot(mixed_out, w_output, preferred_element_type=jnp.float32)
    second = adanorm(
        middle, modulate[2 * model_width : 3 * model_width], modulate[3 * model_width :]
    ).astype(jnp.bfloat16)
    upward = jnp.dot(second, w_up, preferred_element_type=jnp.float32)
    gated_up = jax.nn.silu(upward).astype(jnp.bfloat16)
    final_rows = middle + jnp.dot(gated_up, w_down, preferred_element_type=jnp.float32)
    picked = (
        (final_rows[decode_idx[0]] + final_rows[decode_idx[1]] + final_rows[decode_idx[2]]) / 3.0
    ).astype(jnp.bfloat16)
    output = jnp.einsum("pd,dc->cp", picked, w_decode, preferred_element_type=jnp.float32)
    predicted = c_skip * noisy_in + c_out * output
    stored = (
        inputs,
        start_rows,
        modulate,
        normed,
        project,
        extended,
        attention,
        mixed_out,
        middle,
        second,
        upward,
        gated_up,
        picked,
        waves,
        c_in,
        c_skip,
        c_out,
    )
    return (predicted, stored)


def backward(gathered, stored, d_pred, owner_hot, counted, decode_idx, near_idx, send_idx):
    w_encode, w_project, w_output, w_up, w_down, w_noise, w_decode = gathered
    (
        inputs,
        start_rows,
        modulate,
        normed,
        project,
        extended,
        attention,
        mixed_out,
        middle,
        second,
        upward,
        gated_up,
        picked,
        waves,
        c_in,
        c_skip,
        c_out,
    ) = stored
    model_width = w_project.shape[0]
    node_rows = near_idx.shape[0]
    halo_rows = send_idx.shape[0] // 2
    d_output = (c_out * d_pred).astype(jnp.bfloat16)
    g_decode = jnp.einsum("pd,cp->dc", picked, d_output, preferred_element_type=jnp.float32)
    dpicked = jnp.einsum("cp,dc->pd", d_output, w_decode, preferred_element_type=jnp.float32) / 3.0
    dfinal = jnp.zeros(middle.shape, jnp.float32).at[decode_idx[0]].add(dpicked)
    dfinal = dfinal.at[decode_idx[1]].add(dpicked).at[decode_idx[2]].add(dpicked)
    dbranch = dfinal.astype(jnp.bfloat16)
    g_down = jnp.einsum("nf,nd->fd", gated_up, dbranch, preferred_element_type=jnp.float32)
    dgated = jnp.einsum("nd,fd->nf", dbranch, w_down, preferred_element_type=jnp.float32)
    dupward = jax.vjp(jax.nn.silu, upward)[1](dgated)[0].astype(jnp.bfloat16)
    g_up = jnp.einsum("nd,nf->df", second, dupward, preferred_element_type=jnp.float32)
    dsecond = jnp.einsum("nf,df->nd", dupward, w_up, preferred_element_type=jnp.float32)
    pull_two = jax.vjp(
        adanorm, middle, modulate[2 * model_width : 3 * model_width], modulate[3 * model_width :]
    )[1]
    dmid_norm, dscale_two, dshift_two = pull_two(dsecond)
    dmiddle = dfinal + dmid_norm
    d_attn = dmiddle.astype(jnp.bfloat16)
    g_output = jnp.einsum("nd,ne->de", mixed_out, d_attn, preferred_element_type=jnp.float32)
    dmixed = (
        jnp.einsum("ne,de->nd", d_attn, w_output, preferred_element_type=jnp.float32)
        .astype(jnp.bfloat16)
        .reshape(-1, HEADS, HD)
    )
    key_rows, val_rows = split_near(extended, near_idx, model_width)
    queries = project[:, :model_width].reshape(-1, HEADS, HD)
    d_probs = jnp.einsum("nhd,njhd->nhj", dmixed, val_rows, preferred_element_type=jnp.float32)
    dvalues = jnp.einsum(
        "nhj,nhd->njhd", attention.astype(jnp.bfloat16), dmixed, preferred_element_type=jnp.float32
    )
    dscores = attention * (d_probs - jnp.sum(attention * d_probs, axis=-1, keepdims=True))
    dscore_low = (dscores * HD ** (-0.5)).astype(jnp.bfloat16)
    dqueries = jnp.einsum("nhj,njhd->nhd", dscore_low, key_rows, preferred_element_type=jnp.float32)
    d_keys = jnp.einsum("nhj,nhd->njhd", dscore_low, queries, preferred_element_type=jnp.float32)
    d_near = jnp.concatenate(
        [
            d_keys.reshape(node_rows, NEIGH, model_width),
            dvalues.reshape(node_rows, NEIGH, model_width),
        ],
        axis=-1,
    )
    dextended = jnp.zeros(extended.shape, jnp.float32).at[near_idx].add(d_near)
    returned = padded(dextended[node_rows:].astype(jnp.bfloat16), (("patch", 0),), halo_rows)
    dkeyval = (
        dextended[:node_rows].at[send_idx[:halo_rows]].add(returned[:halo_rows].astype(jnp.float32))
    )
    dkeyval = dkeyval.at[send_idx[halo_rows:]].add(returned[3 * halo_rows :].astype(jnp.float32))
    dproject = jnp.concatenate([dqueries.reshape(node_rows, model_width), dkeyval], axis=1).astype(
        jnp.bfloat16
    )
    g_project = jnp.einsum("nd,ne->de", normed, dproject, preferred_element_type=jnp.float32)
    dnormed = jnp.einsum("ne,de->nd", dproject, w_project, preferred_element_type=jnp.float32)
    pull_one = jax.vjp(
        adanorm, start_rows, modulate[:model_width], modulate[model_width : 2 * model_width]
    )[1]
    dstart_norm, dscale_one, dshift_one = pull_one(dnormed)
    dstart = dmiddle + dstart_norm
    dsummed = (dstart / counted[:, None]).astype(jnp.bfloat16)
    dencoded = jnp.einsum(
        "np,nd->pd", owner_hot, dsummed, preferred_element_type=jnp.float32
    ).astype(jnp.bfloat16)
    g_encode = jnp.einsum("cp,pd->cd", inputs, dencoded, preferred_element_type=jnp.float32)
    dinputs = jnp.einsum("pd,cd->cp", dencoded, w_encode, preferred_element_type=jnp.float32)
    dmodulate = jnp.concatenate([dscale_one, dshift_one, dscale_two, dshift_two])
    g_noise = waves[:, None] * dmodulate[None, :]
    channels = d_pred.shape[0]
    dnoisy = c_skip * d_pred + c_in * dinputs[channels:]
    return ((g_encode, g_project, g_output, g_up, g_down, g_noise, g_decode), dnoisy)


def on_device(
    previous_state,
    target_state,
    noise_draws,
    noise_level,
    pixel_owner,
    mesh_to_grid,
    neighbours,
    halo_send,
    node_count,
    pixel_count,
    w_encode,
    w_project,
    w_output,
    w_up,
    w_down,
    w_noise,
    w_decode,
    m_encode,
    m_project,
    m_output,
    m_up,
    m_down,
    m_noise,
    m_decode,
    v_encode,
    v_project,
    v_output,
    v_up,
    v_down,
    v_noise,
    v_decode,
):
    low_encode = w_encode.astype(jnp.bfloat16)
    low_project = w_project.astype(jnp.bfloat16)
    low_output = w_output.astype(jnp.bfloat16)
    low_up = w_up.astype(jnp.bfloat16)
    low_down = w_down.astype(jnp.bfloat16)
    low_noise = w_noise.astype(jnp.bfloat16)
    low_decode = w_decode.astype(jnp.bfloat16)
    gathered = (
        lax.all_gather(low_encode, ("patch", "rep"), axis=1, tiled=True),
        lax.all_gather(low_project, ("patch", "rep"), axis=0, tiled=True),
        lax.all_gather(low_output, ("patch", "rep"), axis=0, tiled=True),
        lax.all_gather(low_up, ("patch", "rep"), axis=0, tiled=True),
        lax.all_gather(low_down, ("patch", "rep"), axis=0, tiled=True),
        lax.all_gather(low_noise, ("patch", "rep"), axis=1, tiled=True),
        lax.all_gather(low_decode, ("patch", "rep"), axis=0, tiled=True),
    )
    previous = previous_state[0]
    target = target_state[0]
    noise_now = noise_draws[0]
    levels = noise_level[0]
    owners = pixel_owner[0]
    decode_idx = mesh_to_grid[0]
    near_idx = neighbours[0]
    send_idx = halo_send[0]
    node_rows = near_idx.shape[0]
    pixels = owners.shape[0]
    pixel_live = (jnp.arange(pixels) < pixel_count[0, 0]).astype(jnp.float32)
    node_live = jnp.arange(node_rows) < node_count[0, 0]
    owner_hot = (
        (owners[None, :] == jnp.arange(node_rows)[:, None]) & (pixel_live[None, :] > 0.0)
    ).astype(jnp.bfloat16)
    counted = jnp.maximum(jnp.sum(owner_hot, axis=1, dtype=jnp.float32), 1.0)
    valid = (
        (near_idx >= node_rows)
        | node_live[jnp.minimum(near_idx, node_rows - 1)]
        | (jnp.arange(NEIGH)[None, :] == 0)
    )
    pred_one, stored_one = forward(
        gathered,
        target + levels[0] * noise_now[0],
        levels[0],
        previous,
        owner_hot,
        counted,
        decode_idx,
        near_idx,
        valid,
        send_idx,
    )
    pred_two, stored_two = forward(
        gathered,
        pred_one + levels[1] * noise_now[1],
        levels[1],
        previous,
        owner_hot,
        counted,
        decode_idx,
        near_idx,
        valid,
        send_idx,
    )
    error = (pred_two - target) * pixel_live[None, :]
    loss_local = jnp.sum(error * error)
    count_local = previous.shape[0] * jnp.sum(pixel_live)
    grads_two, dnoisy_two = backward(
        gathered, stored_two, 2.0 * error, owner_hot, counted, decode_idx, near_idx, send_idx
    )
    grads_one, _ = backward(
        gathered, stored_one, dnoisy_two, owner_hot, counted, decode_idx, near_idx, send_idx
    )
    grads = [a + b for a, b in zip(grads_one, grads_two)]
    shards = (
        lax.psum_scatter(grads[0], ("patch", "rep"), scatter_dimension=1, tiled=True),
        lax.psum_scatter(grads[1], ("patch", "rep"), scatter_dimension=0, tiled=True),
        lax.psum_scatter(grads[2], ("patch", "rep"), scatter_dimension=0, tiled=True),
        lax.psum_scatter(grads[3], ("patch", "rep"), scatter_dimension=0, tiled=True),
        lax.psum_scatter(grads[4], ("patch", "rep"), scatter_dimension=0, tiled=True),
        lax.psum_scatter(grads[5], ("patch", "rep"), scatter_dimension=1, tiled=True),
        lax.psum_scatter(grads[6], ("patch", "rep"), scatter_dimension=0, tiled=True),
    )
    squares = jnp.zeros((), jnp.float32)
    for shard in shards:
        squares = squares + jnp.sum(shard * shard)
    totals = lax.psum((squares, loss_local, count_local), ("patch", "rep"))
    grad_norm = jnp.sqrt(totals[0])
    factor = THRESHOLD / jnp.maximum(grad_norm, THRESHOLD)
    masters = (w_encode, w_project, w_output, w_up, w_down, w_noise, w_decode)
    moments = (m_encode, m_project, m_output, m_up, m_down, m_noise, m_decode)
    seconds = (v_encode, v_project, v_output, v_up, v_down, v_noise, v_decode)
    new_weights, new_moments, new_seconds = ([], [], [])
    for w, m, v, g in zip(masters, moments, seconds, shards):
        clipped = g * factor
        moment = BETA_ONE * m + (1.0 - BETA_ONE) * clipped
        variance = BETA_TWO * v + (1.0 - BETA_TWO) * clipped * clipped
        stepped = (
            moment
            / (1.0 - BETA_ONE**STEP)
            / (jnp.sqrt(variance / (1.0 - BETA_TWO**STEP)) + EPSILON)
        )
        new_weights.append(w - LEARN_RATE * (stepped + DECAY_RATE * w))
        new_moments.append(moment)
        new_seconds.append(variance)
    return (
        tuple(new_weights)
        + tuple(new_moments)
        + tuple(new_seconds)
        + (totals[1], totals[2], grad_norm)
    )


def solution(mesh):
    in_specs = (
        P("rep", None, "patch"),
        P("rep", None, "patch"),
        P("rep", None, None, "patch"),
        P("rep", None),
        P("rep", "patch"),
        P("rep", None, "patch"),
        P("rep", "patch", None),
        P("rep", "patch"),
        P("rep", "patch"),
        P("rep", "patch"),
        P(None, ("patch", "rep")),
        P(("patch", "rep"), None),
        P(("patch", "rep"), None),
        P(("patch", "rep"), None),
        P(("patch", "rep"), None),
        P(None, ("patch", "rep")),
        P(("patch", "rep"), None),
        P(None, ("patch", "rep")),
        P(("patch", "rep"), None),
        P(("patch", "rep"), None),
        P(("patch", "rep"), None),
        P(("patch", "rep"), None),
        P(None, ("patch", "rep")),
        P(("patch", "rep"), None),
        P(None, ("patch", "rep")),
        P(("patch", "rep"), None),
        P(("patch", "rep"), None),
        P(("patch", "rep"), None),
        P(("patch", "rep"), None),
        P(None, ("patch", "rep")),
        P(("patch", "rep"), None),
    )
    out_specs = (
        P(None, ("patch", "rep")),
        P(("patch", "rep"), None),
        P(("patch", "rep"), None),
        P(("patch", "rep"), None),
        P(("patch", "rep"), None),
        P(None, ("patch", "rep")),
        P(("patch", "rep"), None),
        P(None, ("patch", "rep")),
        P(("patch", "rep"), None),
        P(("patch", "rep"), None),
        P(("patch", "rep"), None),
        P(("patch", "rep"), None),
        P(None, ("patch", "rep")),
        P(("patch", "rep"), None),
        P(None, ("patch", "rep")),
        P(("patch", "rep"), None),
        P(("patch", "rep"), None),
        P(("patch", "rep"), None),
        P(("patch", "rep"), None),
        P(None, ("patch", "rep")),
        P(("patch", "rep"), None),
        P(),
        P(),
        P(),
    )
    return jax.shard_map(
        on_device, mesh=mesh, in_specs=in_specs, out_specs=out_specs, check_vma=False
    )
```

profile of v0, /device:TPU:0, one launch (start us, length us, event | category | flops | bytes accessed | tf_op | source)
XLA Modules:
  0.0 2108.9 jit_solution(12744505244369265461)
XLA Ops:
  24.4 44.2 %all_gather.21 = bf16[168,512]{0,1:T(8,128)(2,1)S(1)} all-gather(bf16[168,16]{0,1:T(8,128)(2,1)S(1)} %convert_element_type.162), channel_id=1, replica_groups=mesh['patch'=8,'rep'=4] {'patch','rep'}, dimensions={1}, use_global_device_ids=true | all-gather | bytes 177408 | tf_op jit(solution)/shard_map/all_gather | solution.py:260
  74.7 37.4 %all-gather = bf16[32,64,32]{1,2,0:T(8,128)(2,1)S(1)} all-gather(bf16[1,64,32]{1,2,0:T(8,128)(2,1)S(1)} %convert_bitcast_fusion.2), channel_id=1, replica_groups=mesh['patch'=8,'rep'=4] {'patch','rep'}, dimensions={0}, use_global_device_ids=true | all-gather | bytes 135168 | tf_op jit(solution)/shard_map/all_gather | solution.py:265
  114.7 48.3 %gather_fusion = pred[8192]{0:T(1024)(128)(4,1)S(1)} fusion(pred[512]{0:T(512)(128)(4,1)S(1)} %iota_compare_fusion.2, s32[8192]{0:T(1024)S(1)} %broadcast_clamp_fusion.1), kind=kCustom, calls=%fused_computation | custom fusion | bytes 49152 | tf_op jit(solution)/shard_map/gather | solution.py:286
  163.2 42.8 %all_gather.24 = bf16[512,512]{1,0:T(8,128)(2,1)} all-gather(bf16[16,512]{1,0:T(8,128)(2,1)S(1)} %convert_element_type.173), channel_id=1, replica_groups=mesh['patch'=8,'rep'=4] {'patch','rep'}, dimensions={0}, use_global_device_ids=true | all-gather | bytes 540672 | tf_op jit(solution)/shard_map/all_gather | solution.py:262
  220.3 39.5 %all_gather.27 = bf16[512,84]{1,0:T(8,128)(2,1)} all-gather(bf16[16,84]{1,0:T(8,128)(2,1)S(1)} %convert_element_type.179), channel_id=1, replica_groups=mesh['patch'=8,'rep'=4] {'patch','rep'}, dimensions={0}, use_global_device_ids=true | all-gather | bytes 88704 | tf_op jit(solution)/shard_map/all_gather | solution.py:266
  264.4 35.6 %gather_fusion.2 = bf16[8192,1024]{1,0:T(8,128)(2,1)} fusion(bf16[640,1024]{1,0:T(8,128)(2,1)S(1)} %pad_maximum_fusion.4, s32[8192]{0:T(1024)S(1)} %broadcast_clamp_fusion), kind=kCustom, calls=%fused_computation.2 | custom fusion | bytes 33587200 | tf_op jit(solution)/shard_map/gather | solution.py:48
  299.9 13.3 fusion.241
  325.7 5.7 fusion.13
  342.5 12.9 gather_fusion.3
  355.4 12.9 gather_fusion.4
  368.2 13.3 gather_fusion.5
  381.5 9.0 multiply_convert_fusion.1
  410.6 12.7 reshape.532
  432.2 35.6 %gather_fusion.7 = bf16[8192,1024]{1,0:T(8,128)(2,1)} fusion(bf16[640,1024]{1,0:T(8,128)(2,1)S(1)} %pad_maximum_fusion.5, s32[8192]{0:T(1024)S(1)} %broadcast_clamp_fusion), kind=kCustom, calls=%fused_computation.7 | custom fusion | bytes 33587200 | tf_op jit(solution)/shard_map/gather | solution.py:48
  467.8 13.3 fusion.242
  493.5 5.7 fusion.6
  506.5 12.9 gather_fusion.8
  519.4 12.9 gather_fusion.9
  532.2 13.1 gather_fusion.10
  545.3 9.0 multiply_convert_fusion
  561.2 19.9 scatter_custom_fusion
  581.1 20.0 scatter_custom_fusion.1
  601.1 20.4 scatter_custom_fusion.2
  635.5 12.7 reshape.536
  651.8 24.4 %multiply_reduce_fusion.1 = (f32[512,4,16]{1,2,0:T(8,128)}, f32[512,16,4,128]{3,2,1,0:T(4,128)}) fusion(f32[512,4,128]{2,1,0:T(4,128)S(1)} %copy.218, bf16[512,16,4,128]{3,2,1,0:T(4,128)(2,1)} %reshape.536, f32[512,4,16]{1,2,0:T(8,128)} %copy.171), kind=kLoop, calls=%fused_computation.32 | loop fusion | flops 16744448 | bytes 26476544
  683.1 12.7 multiply_bitcast_fusion.3
  695.8 19.9 reshape.540
  715.7 19.9 reshape.541
  735.5 23.4 %pad_maximum_fusion = f32[512,16,1024]{2,1,0:T(8,128)} fusion(f32[512,16,512]{2,1,0:T(8,128)} %reshape.541, f32[512,16,512]{2,1,0:T(8,128)} %reshape.540), kind=kLoop, calls=%fused_computation.29 | loop fusion | flops 8388608 | bytes 67108864 | tf_op jit(solution)/shard_map/concatenate | solution.py:183
  759.0 72.6 %scatter_custom_fusion.3 = f32[640,1024]{1,0:T(8,128)} fusion(s32[8192]{0:T(1024)} %copy-done.94, f32[8192,1024]{1,0:T(8,128)} %bitcast.248, f32[]{:T(128)} %constant.40.clone.1), kind=kCustom, calls=%fused_computation.137 | custom fusion | flops 8388608 | bytes 2621952 | tf_op jit(solution)/shard_map/scatter-add | solution.py:190
  869.5 19.9 scatter_custom_fusion.6
  889.3 20.4 scatter_custom_fusion.7
  909.8 20.0 scatter_custom_fusion.8
  948.7 24.7 %multiply_reduce_fusion = (f32[512,4,16]{1,2,0:T(8,128)}, f32[512,16,4,128]{3,2,1,0:T(4,128)}) fusion(f32[512,4,128]{2,1,0:T(4,128)} %copy.219, bf16[512,16,4,128]{3,2,1,0:T(4,128)(2,1)} %reshape.532, f32[512,4,16]{1,2,0:T(8,128)} %copy.177), kind=kLoop, calls=%fused_computation.31 | loop fusion | flops 16744448 | bytes 26476544
  979.7 12.6 multiply_bitcast_fusion.1
  992.3 19.9 reshape.544
  1012.2 19.9 reshape.545
  1032.0 23.4 %pad_maximum_fusion.1 = f32[512,16,1024]{2,1,0:T(8,128)} fusion(f32[512,16,512]{2,1,0:T(8,128)} %reshape.545, f32[512,16,512]{2,1,0:T(8,128)} %reshape.544), kind=kLoop, calls=%fused_computation.30 | loop fusion | flops 8388608 | bytes 67108864 | tf_op jit(solution)/shard_map/concatenate | solution.py:183
  1055.5 72.5 %scatter_custom_fusion.9 = f32[640,1024]{1,0:T(8,128)} fusion(s32[8192]{0:T(1024)} %copy-done.94, f32[8192,1024]{1,0:T(8,128)} %bitcast.247, f32[]{:T(128)} %constant.40.clone.1), kind=kCustom, calls=%fused_computation.135 | custom fusion | flops 8388608 | bytes 2621952 | tf_op jit(solution)/shard_map/scatter-add | solution.py:190
  1171.2 7.1 fusion.113
  1210.1 57.7 %reduce-scatter.20.cloned.1.call-done = f32[16,84]{1,0:T(8,128)} async-done(((f32[512,84]{1,0:T(8,128)}), f32[16,84]{1,0:T(8,128)}) %reduce-scatter.20.cloned.1.call-update) | async-done | bytes 5392 | tf_op jit(solution)/shard_map/reduce_scatter | solution.py:330
  1269.1 131.6 %reduce-scatter.22.cloned.1.call-done = f32[64,32]{1,0:T(8,128)} async-done(((f32[2048,32]{1,0:T(8,128)}), f32[64,32]{1,0:T(8,128)}) %reduce-scatter.22.cloned.1.call-update) | async-done | bytes 8208
  1402.1 130.5 %reduce-scatter.10.cloned.1.call-done = f32[168,16]{0,1:T(8,128)} async-done(((f32[168,512]{0,1:T(8,128)}), f32[168,16]{0,1:T(8,128)}) %reduce-scatter.10.cloned.1.call-update) | async-done | bytes 10768 | tf_op jit(solution)/shard_map/reduce_scatter | solution.py:324
  1534.0 131.7 %reduce-scatter.14.cloned.1.call-done = f32[16,512]{1,0:T(8,128)} async-done(((f32[512,512]{1,0:T(8,128)}), f32[16,512]{1,0:T(8,128)}) %reduce-scatter.14.cloned.1.call-update) | async-done | bytes 32784 | tf_op jit(solution)/shard_map/reduce_scatter | solution.py:326
  1667.0 101.6 %reduce-scatter.12.cloned.1.call-done = f32[16,1536]{1,0:T(8,128)} async-done(((f32[512,1536]{1,0:T(8,128)}), f32[16,1536]{1,0:T(8,128)}) %reduce-scatter.12.cloned.1.call-update) | async-done | bytes 98320 | tf_op jit(solution)/shard_map/reduce_scatter | solution.py:325
  1772.1 138.8 %reduce-scatter.16.cloned.1.call-done = f32[16,2048]{1,0:T(8,128)} async-done(((f32[512,2048]{1,0:T(8,128)}), f32[16,2048]{1,0:T(8,128)}) %reduce-scatter.16.cloned.1.call-update) | async-done | bytes 131088 | tf_op jit(solution)/shard_map/reduce_scatter | solution.py:327
  1913.1 136.8 %reduce-scatter.18.cloned.1.call-done = f32[64,512]{1,0:T(8,128)} async-done(((f32[2048,512]{1,0:T(8,128)}), f32[64,512]{1,0:T(8,128)}) %reduce-scatter.18.cloned.1.call-update) | async-done | bytes 131088 | tf_op jit(solution)/shard_map/reduce_scatter | solution.py:328
  2053.4 37.1 %all-reduce = (f32[]{:T(128)}, f32[]{:T(128)}, f32[]{:T(128)}) all-reduce(f32[]{:T(128)S(6)} %add.514, f32[]{:T(128)} %get-tuple-element.72, f32[]{:T(128)S(6)} %mul_shard_map.3), channel_id=1, replica_groups=mesh['patch'=8,'rep'=4] {'patch','rep'}, use_global_device_ids=true, to_apply=%region_57.58 | all-reduce | flops 3 | bytes 24 | tf_op jit(solution)/shard_map/psum | solution.py:335
  (571 shorter events, 295.6 us)
Async XLA Ops:
  7.2 200.5 %all-gather.5.cloned.1.call-start = ((), (), s32[]{:S(2)}) async-start(), calls=%async_computation.7 | async-start | bytes 1622016 | tf_op jit(solution)/shard_map/all_gather | solution.py:261
  8.9 323.5 %all-gather.7.cloned.1.call-start = ((), (), s32[]{:S(2)}) async-start(), calls=%async_computation.8 | async-start | bytes 2162688 | tf_op jit(solution)/shard_map/all_gather | solution.py:263
  10.5 327.2 %all-gather.9.cloned.1.call-start = ((), (), s32[]{:S(2)}) async-start(), calls=%async_computation.9 | async-start | bytes 2162688 | tf_op jit(solution)/shard_map/all_gather | solution.py:264
  12.1 1255.7 %reduce-scatter.20.cloned.1.call-start = ((), (), s32[]{:S(2)}) async-start(), calls=%async_computation.15 | async-start | bytes 270336 | tf_op jit(solution)/shard_map/reduce_scatter | solution.py:330
  74.4 257.2 %copy-start.10 = (f32[512,512]{0,1:T(8,128)}, f32[512,512]{0,1:T(8,128)S(1)}, u32[]{:S(2)}) copy-start(f32[512,512]{0,1:T(8,128)S(1)} %get-tuple-element.104) | copy-start | bytes 3145732
  74.5 133.3 %copy-start.107 = (f32[512]{0:T(512)}, f32[512]{0:T(512)S(1)}, u32[]{:S(2)}) copy-start(f32[512]{0:T(512)S(1)} %broadcast_multiply_fusion.3) | copy-start | bytes 6148
  112.8 219.6 %copy-start.84 = (f32[512]{0:T(512)}, f32[512]{0:T(512)S(1)}, u32[]{:S(2)}) copy-start(f32[512]{0:T(512)S(1)} %get-tuple-element.95) | copy-start | bytes 6148
  112.8 219.6 %copy-start.99 = (f32[512]{0:T(512)}, f32[512]{0:T(512)S(1)}, u32[]{:S(2)}) copy-start(f32[512]{0:T(512)S(1)} %get-tuple-element.96) | copy-start | bytes 6148
  212.6 50.1 %collective-permute-start = (bf16[64,1024]{1,0:T(8,128)(2,1)S(1)}, bf16[64,1024]{1,0:T(8,128)(2,1)S(1)}, u32[]{:S(2)}, u32[]{:S(2)}) collective-permute-start(bf16[64,1024]{1,0:T(8,128)(2,1)S(1)} %get-tuple-element.80), channel_id=1, source_target_pairs={{0,4},{4,8},{8,12},{12,16},{16,20},{20,24},{24,28},{28,0},{1,5},{5... | collective-permute-start | bytes 393224 | tf_op jit(solution)/shard_map/ppermute | solution.py:28
  212.6 50.6 %collective-permute-start.1 = (bf16[64,1024]{1,0:T(8,128)(2,1)S(1)}, bf16[64,1024]{1,0:T(8,128)(2,1)}, u32[]{:S(2)}, u32[]{:S(2)}) collective-permute-start(bf16[64,1024]{1,0:T(8,128)(2,1)S(1)} %get-tuple-element.81), channel_id=1, source_target_pairs={{4,0},{8,4},{12,8},{16,12},{20,16},{24,20},{28,24},{0,28},{5,1},{9... | collective-permute-start | bytes 393224 | tf_op jit(solution)/shard_map/ppermute | solution.py:29
  218.1 181.1 %copy-start.101 = (f32[512]{0:T(512)}, f32[512]{0:T(512)S(1)}, u32[]{:S(2)}) copy-start(f32[512]{0:T(512)S(1)} %get-tuple-element.94) | copy-start | bytes 6148
  218.1 181.1 %copy-start.116 = (f32[512]{0:T(512)}, f32[512]{0:T(512)S(1)}, u32[]{:S(2)}) copy-start(f32[512]{0:T(512)S(1)} %get-tuple-element.93) | copy-start | bytes 6148
  403.3 27.4 %collective-permute-start.2 = (bf16[64,1024]{1,0:T(8,128)(2,1)}, bf16[64,1024]{1,0:T(8,128)(2,1)}, u32[]{:S(2)}, u32[]{:S(2)}) collective-permute-start(bf16[64,1024]{1,0:T(8,128)(2,1)} %get-tuple-element.78), channel_id=1, source_target_pairs={{0,4},{4,8},{8,12},{12,16},{16,20},{20,24},{24,28},{28,0},{1,5},{5... | collective-permute-start | bytes 393224 | tf_op jit(solution)/shard_map/ppermute | solution.py:28
  403.4 27.4 %collective-permute-start.3 = (bf16[64,1024]{1,0:T(8,128)(2,1)}, bf16[64,1024]{1,0:T(8,128)(2,1)}, u32[]{:S(2)}, u32[]{:S(2)}) collective-permute-start(bf16[64,1024]{1,0:T(8,128)(2,1)} %get-tuple-element.79), channel_id=1, source_target_pairs={{4,0},{8,4},{12,8},{16,12},{20,16},{24,20},{28,24},{0,28},{5,1},{9... | collective-permute-start | bytes 393224 | tf_op jit(solution)/shard_map/ppermute | solution.py:29
  500.0 133.3 %copy-start = (f32[512,512]{0,1:T(8,128)}, f32[512,512]{0,1:T(8,128)S(1)}, u32[]{:S(2)}) copy-start(f32[512,512]{0,1:T(8,128)S(1)} %get-tuple-element.112) | copy-start | bytes 3145732
  500.0 133.3 %copy-start.76 = (f32[512]{0:T(512)}, f32[512]{0:T(512)S(1)}, u32[]{:S(2)}) copy-start(f32[512]{0:T(512)S(1)} %broadcast_multiply_fusion) | copy-start | bytes 6148
  834.2 11.5 collective-permute-start.4
  834.2 14.5 collective-permute-start.5
  1136.1 264.6 %reduce-scatter.22.cloned.1.call-start = ((), (), s32[]{:S(2)}) async-start(), calls=%async_computation.16 | async-start | bytes 1081344
  1137.8 12.5 collective-permute-start.6
  1137.8 16.6 collective-permute-start.7
  1171.2 361.4 %reduce-scatter.10.cloned.1.call-start = ((), (), s32[]{:S(2)}) async-start(), calls=%async_computation.10 | async-start | bytes 540672 | tf_op jit(solution)/shard_map/reduce_scatter | solution.py:324
  1182.9 482.8 %reduce-scatter.14.cloned.1.call-start = ((), (), s32[]{:S(2)}) async-start(), calls=%async_computation.12 | async-start | bytes 1081344 | tf_op jit(solution)/shard_map/reduce_scatter | solution.py:326
  1187.6 581.1 %reduce-scatter.12.cloned.1.call-start = ((), (), s32[]{:S(2)}) async-start(), calls=%async_computation.11 | async-start | bytes 3244032 | tf_op jit(solution)/shard_map/reduce_scatter | solution.py:325
  1193.0 717.9 %reduce-scatter.16.cloned.1.call-start = ((), (), s32[]{:S(2)}) async-start(), calls=%async_computation.13 | async-start | bytes 4325376 | tf_op jit(solution)/shard_map/reduce_scatter | solution.py:327
  1200.1 849.8 %reduce-scatter.18.cloned.1.call-start = ((), (), s32[]{:S(2)}) async-start(), calls=%async_computation.14 | async-start | bytes 4325376 | tf_op jit(solution)/shard_map/reduce_scatter | solution.py:328
  1208.6 882.7 %copy-start.110 = (f32[32,64]{1,0:T(8,128)S(1)}, f32[32,64]{1,0:T(8,128)}, u32[]{:S(2)}) copy-start(f32[32,64]{1,0:T(8,128)} %param.46) | copy-start | bytes 24580
  1208.6 882.7 %copy-start.136 = (f32[32,64]{1,0:T(8,128)S(1)}, f32[32,64]{1,0:T(8,128)}, u32[]{:S(2)}) copy-start(f32[32,64]{1,0:T(8,128)} %param.53) | copy-start | bytes 24580
  1208.6 882.8 %copy-start.137 = (f32[32,64]{1,0:T(8,128)S(1)}, f32[32,64]{1,0:T(8,128)}, u32[]{:S(2)}) copy-start(f32[32,64]{1,0:T(8,128)} %param.60) | copy-start | bytes 24580
  1208.6 883.4 %copy-start.125 = (f32[16,84]{1,0:T(8,128)S(1)}, f32[16,84]{1,0:T(8,128)}, u32[]{:S(2)}) copy-start(f32[16,84]{1,0:T(8,128)} %param.47) | copy-start | bytes 16132
  1208.6 883.4 %copy-start.141 = (f32[16,84]{1,0:T(8,128)S(1)}, f32[16,84]{1,0:T(8,128)}, u32[]{:S(2)}) copy-start(f32[16,84]{1,0:T(8,128)} %param.54) | copy-start | bytes 16132
  1208.6 883.4 %copy-start.142 = (f32[16,84]{1,0:T(8,128)S(1)}, f32[16,84]{1,0:T(8,128)}, u32[]{:S(2)}) copy-start(f32[16,84]{1,0:T(8,128)} %param.61) | copy-start | bytes 16132
  1208.6 884.7 %copy-start.66 = (f32[64,512]{1,0:T(8,128)S(1)}, f32[64,512]{1,0:T(8,128)}, u32[]{:S(2)}) copy-start(f32[64,512]{1,0:T(8,128)} %param.45) | copy-start | bytes 393220
  1208.6 884.7 %copy-start.86 = (f32[64,512]{1,0:T(8,128)S(1)}, f32[64,512]{1,0:T(8,128)}, u32[]{:S(2)}) copy-start(f32[64,512]{1,0:T(8,128)} %param.52) | copy-start | bytes 393220
  1208.6 884.7 %copy-start.87 = (f32[64,512]{1,0:T(8,128)S(1)}, f32[64,512]{1,0:T(8,128)}, u32[]{:S(2)}) copy-start(f32[64,512]{1,0:T(8,128)} %param.59) | copy-start | bytes 393220
  1208.7 886.4 %copy-start.67 = (f32[16,2048]{1,0:T(8,128)S(1)}, f32[16,2048]{1,0:T(8,128)}, u32[]{:S(2)}) copy-start(f32[16,2048]{1,0:T(8,128)} %param.44) | copy-start | bytes 393220
  1208.7 886.4 %copy-start.88 = (f32[16,2048]{1,0:T(8,128)S(1)}, f32[16,2048]{1,0:T(8,128)}, u32[]{:S(2)}) copy-start(f32[16,2048]{1,0:T(8,128)} %param.51) | copy-start | bytes 393220
  1208.7 886.4 %copy-start.89 = (f32[16,2048]{1,0:T(8,128)S(1)}, f32[16,2048]{1,0:T(8,128)}, u32[]{:S(2)}) copy-start(f32[16,2048]{1,0:T(8,128)} %param.58) | copy-start | bytes 393220
  1208.7 888.1 %copy-start.93 = (f32[16,512]{1,0:T(8,128)S(1)}, f32[16,512]{1,0:T(8,128)}, u32[]{:S(2)}) copy-start(f32[16,512]{1,0:T(8,128)} %param.43) | copy-start | bytes 98308
  1208.7 888.1 %copy-start.122 = (f32[16,512]{1,0:T(8,128)S(1)}, f32[16,512]{1,0:T(8,128)}, u32[]{:S(2)}) copy-start(f32[16,512]{1,0:T(8,128)} %param.50) | copy-start | bytes 98308
  1208.7 888.1 %copy-start.123 = (f32[16,512]{1,0:T(8,128)S(1)}, f32[16,512]{1,0:T(8,128)}, u32[]{:S(2)}) copy-start(f32[16,512]{1,0:T(8,128)} %param.57) | copy-start | bytes 98308
  1208.7 889.5 %copy-start.73 = (f32[16,1536]{1,0:T(8,128)S(1)}, f32[16,1536]{1,0:T(8,128)}, u32[]{:S(2)}) copy-start(f32[16,1536]{1,0:T(8,128)} %param.42) | copy-start | bytes 294916
  1208.7 889.5 %copy-start.103 = (f32[16,1536]{1,0:T(8,128)S(1)}, f32[16,1536]{1,0:T(8,128)}, u32[]{:S(2)}) copy-start(f32[16,1536]{1,0:T(8,128)} %param.49) | copy-start | bytes 294916
  1208.8 889.5 %copy-start.104 = (f32[16,1536]{1,0:T(8,128)S(1)}, f32[16,1536]{1,0:T(8,128)}, u32[]{:S(2)}) copy-start(f32[16,1536]{1,0:T(8,128)} %param.56) | copy-start | bytes 294916
  1208.8 891.1 %copy-start.112 = (f32[168,16]{0,1:T(8,128)S(1)}, f32[168,16]{0,1:T(8,128)}, u32[]{:S(2)}) copy-start(f32[168,16]{0,1:T(8,128)} %param.41) | copy-start | bytes 32260
  1208.8 891.1 %copy-start.138 = (f32[168,16]{0,1:T(8,128)S(1)}, f32[168,16]{0,1:T(8,128)}, u32[]{:S(2)}) copy-start(f32[168,16]{0,1:T(8,128)} %param.48) | copy-start | bytes 32260
  1208.8 891.1 %copy-start.139 = (f32[168,16]{0,1:T(8,128)S(1)}, f32[168,16]{0,1:T(8,128)}, u32[]{:S(2)}) copy-start(f32[168,16]{0,1:T(8,128)} %param.55) | copy-start | bytes 32260
  1532.6 567.3 %copy-start.113 = (f32[168,16]{0,1:T(8,128)S(1)}, f32[168,16]{0,1:T(8,128)}, u32[]{:S(2)}) copy-start(f32[168,16]{0,1:T(8,128)} %reduce-scatter.10.cloned.1.call-done) | copy-start | bytes 32260
  (138 other events, 1573.9 us)
Sparse Core Ops, SparseCore 0:
  11.5 57.6 all-gather.4
  72.7 55.7 all-gather.6
  131.9 55.9 all-gather.8
  1136.2 131.5 reduce-scatter.19
  1270.0 130.6 reduce-scatter.21
  1402.8 129.7 reduce-scatter.9
  1534.9 130.7 reduce-scatter.13
  1671.1 97.4 reduce-scatter.11
  1770.9 139.9 reduce-scatter.15
  1913.0 136.8 reduce-scatter.17
where the time goes:
time: 2120 us; the launch traced here: 2110 us
  waiting for transfers between devices  829 us (39%)
  other arithmetic  471 us (22%)
  local copies, waits for them, and re-layouts  418 us (20%)
  blocking collectives  201 us (9%)
  matrix products  139 us (7%)
  between operations  31 us (1%)
    scatter-add x2, other arithmetic, backward(): dextended = jnp.zeros(extended.shape, jnp.float32).at[near_idx].add(d_near)  145 us
    reduce_scatter x1, waiting for transfers between devices, on_device(): lax.psum_scatter(grads[3], ('patch', 'rep'), scatter_dimension=0, tiled=T...  139 us
    reduce_scatter x1, waiting for transfers between devices, on_device(): lax.psum_scatter(grads[4], ('patch', 'rep'), scatter_dimension=0, tiled=T...  137 us
    unnamed x11, waiting for transfers between devices  132 us
    reduce_scatter x1, waiting for transfers between devices, on_device(): lax.psum_scatter(grads[2], ('patch', 'rep'), scatter_dimension=0, tiled=T...  132 us
    reduce_scatter x1, waiting for transfers between devices, on_device(): lax.psum_scatter(grads[0], ('patch', 'rep'), scatter_dimension=1, tiled=T...  130 us
    reduce_scatter x1, waiting for transfers between devices, on_device(): lax.psum_scatter(grads[1], ('patch', 'rep'), scatter_dimension=0, tiled=T...  102 us
    scatter-add x4, other arithmetic, backward(): dfinal.at[decode_idx[1]].add(dpicked).at[decode_idx[2]].add(dpicked)  81 us
  transfers between devices with their start and end apart: 18, of which 7 were waited for; matrix products, arithmetic and copies ran while one was open for 12% of the time, Pallas kernels for 0%

commit v1 on v0

v1 whole, which is shorter than its diff:
```python
import jax
import jax.numpy as jnp
from jax import lax
from jax.sharding import PartitionSpec as P

HEADS = 4
HD = 128
FOUR = 32
NEIGH = 16
STEP = 5


LEARN_RATE = 0.03
BETA_ONE = 0.9
BETA_TWO = 0.95
EPSILON = 1e-08
DECAY_RATE = 0.1
THRESHOLD = 1.0

BOTH = ("patch", "rep")
LOW = jnp.bfloat16
WIDE = jnp.float32
SCALE = HD ** (-0.5)


def nn(a, b):
    return lax.dot_general(a, b, (((1,), (0,)), ((), ())), preferred_element_type=WIDE)


def nt(a, b):
    return lax.dot_general(a, b, (((1,), (1,)), ((), ())), preferred_element_type=WIDE)


def tn(a, b):
    return lax.dot_general(a, b, (((0,), (0,)), ((), ())), preferred_element_type=WIDE)


def tt(a, b):
    return lax.dot_general(a, b, (((0,), (1,)), ((), ())), preferred_element_type=WIDE)


def fourier(level):
    frequency = 0.25 * (jnp.arange(FOUR // 2).astype(jnp.float32) + 1.0)
    angles = jnp.log(level) * frequency
    return jnp.concatenate([jnp.sin(angles), jnp.cos(angles)])


def norm_parts(hidden):
    centre = hidden - jnp.mean(hidden, axis=-1, keepdims=True)
    spread = jnp.mean(centre * centre, axis=-1, keepdims=True)
    inverse = lax.rsqrt(spread + 1e-05)
    return centre * inverse, inverse


def norm_back(unit, inverse, scaling, d_out):
    d_scale = jnp.sum(d_out * unit, axis=0)
    d_shift = jnp.sum(d_out, axis=0)
    d_unit = d_out * (1.0 + scaling)
    along = jnp.mean(d_unit * unit, axis=-1, keepdims=True)
    d_hidden = inverse * (d_unit - jnp.mean(d_unit, axis=-1, keepdims=True) - unit * along)
    return d_hidden, d_scale, d_shift


def exchange(rows):
    half = rows.shape[0] // 2
    devices = lax.axis_size("patch")
    up = [(i, (i + 1) % devices) for i in range(devices)]
    down = [(j, i) for i, j in up]
    from_lower = lax.ppermute(rows[half:], "patch", up)
    from_upper = lax.ppermute(rows[:half], "patch", down)
    return jnp.concatenate([from_lower, from_upper], axis=0)


def attend(project, extended, listed, head):
    width = HEADS * HD
    cols = slice(head * HD, (head + 1) * HD)
    queries, keys = project[:, cols], extended[:, cols]
    values = extended[:, width + head * HD : width + (head + 1) * HD]
    scores = jnp.where(listed > 0.0, nt(queries, keys) * SCALE, -1e30)
    top = jnp.max(scores, axis=-1, keepdims=True)
    weight = listed * jnp.exp(scores - top)
    return queries, keys, values, weight / jnp.sum(weight, axis=-1, keepdims=True)


def forward(weights, wave, noisy, level, sums_previous, shared):
    w_encode, w_project, w_output, w_up, w_down, w_decode = weights
    owner_hot, counted, node_hot, listed, send_hot = shared
    width = w_project.shape[0]
    c_in = lax.rsqrt(level * level + 1.0)
    c_skip = 1.0 / (level * level + 1.0)
    c_out = level * c_in
    sums = jnp.concatenate([sums_previous, nt(owner_hot, (noisy * c_in).astype(LOW))], axis=1).astype(LOW)
    start = nt(sums, w_encode) / counted
    unit_one, inv_one = norm_parts(start)
    normed = (unit_one * (1.0 + wave[0]) + wave[1]).astype(LOW)
    project = nn(normed, w_project).astype(LOW)
    keyval = project[:, width:]
    extended = jnp.concatenate([keyval, exchange(nn(send_hot, keyval).astype(LOW))], axis=0)
    mixed, attention = [], []
    for head in range(HEADS):
        _, _, values, probs = attend(project, extended, listed, head)
        attention.append(probs)
        mixed.append(nn(probs.astype(LOW), values))
    mixed = jnp.concatenate(mixed, axis=1).astype(LOW)
    middle = start + nn(mixed, w_output)
    unit_two, inv_two = norm_parts(middle)
    second = (unit_two * (1.0 + wave[2]) + wave[3]).astype(LOW)
    upward = nn(second, w_up)
    gated = (upward * jax.nn.sigmoid(upward)).astype(LOW)
    final = (middle + nn(gated, w_down)).astype(LOW)
    nodes_out = tt(w_decode, final).astype(LOW)
    output = nn(nodes_out, node_hot) * (1.0 / 3.0)
    predicted = c_skip * noisy + c_out * output
    stored = (sums, unit_one, inv_one, normed, project, extended, attention, mixed, unit_two, inv_two, second,
              upward, gated, final, c_in, c_skip, c_out)
    return predicted, stored


def backward(weights, wave, stored, d_pred, shared, need_input):
    w_encode, w_project, w_output, w_up, w_down, w_decode = weights
    owner_hot, counted, node_hot, listed, send_hot = shared
    (sums, unit_one, inv_one, normed, project, extended, attention, mixed, unit_two, inv_two, second,
     upward, gated, final, c_in, c_skip, c_out) = stored
    width = w_project.shape[0]
    nodes = project.shape[0]
    d_output = (c_out * d_pred).astype(LOW)
    gathered = (nt(node_hot, d_output) * (1.0 / 3.0)).astype(LOW)
    g_decode = tn(final, gathered)
    d_final = nt(gathered, w_decode)
    d_branch = d_final.astype(LOW)
    g_down = tn(gated, d_branch)
    d_gated = nt(d_branch, w_down)
    gate = jax.nn.sigmoid(upward)
    d_upward = (d_gated * gate * (1.0 + upward * (1.0 - gate))).astype(LOW)
    g_up = tn(second, d_upward)
    d_second = nt(d_upward, w_up)
    d_norm, d_scale_two, d_shift_two = norm_back(unit_two, inv_two, wave[2], d_second)
    d_middle = d_final + d_norm
    d_attn = d_middle.astype(LOW)
    g_output = tn(mixed, d_attn)
    d_mixed = nt(d_attn, w_output).astype(LOW)
    d_queries, d_keys, d_values = [], [], []
    for head in range(HEADS):
        cols = slice(head * HD, (head + 1) * HD)
        queries, keys = project[:, cols], extended[:, cols]
        values = extended[:, width + head * HD : width + (head + 1) * HD]
        probs = attention[head]
        d_head = d_mixed[:, cols]
        d_probs = nt(d_head, values)
        d_values.append(tn(probs.astype(LOW), d_head))
        d_scores = probs * (d_probs - jnp.sum(probs * d_probs, axis=-1, keepdims=True))
        d_low = (d_scores * SCALE).astype(LOW)
        d_queries.append(nn(d_low, keys))
        d_keys.append(tn(d_low, queries))
    d_extended = jnp.concatenate(d_keys + d_values, axis=1)
    returned = exchange_order(d_extended[nodes:].astype(LOW))
    d_keyval = d_extended[:nodes] + tn(send_hot, returned)
    d_project = jnp.concatenate(d_queries + [d_keyval], axis=1).astype(LOW)
    g_project = tn(normed, d_project)
    d_normed = nt(d_project, w_project)
    d_norm, d_scale_one, d_shift_one = norm_back(unit_one, inv_one, wave[0], d_normed)
    d_start = d_middle + d_norm
    d_summed = (d_start / counted).astype(LOW)
    g_encode = tn(d_summed, sums)
    d_wave = jnp.concatenate([d_scale_one, d_shift_one, d_scale_two, d_shift_two])
    grads = [g_encode, g_project, g_output, g_up, g_down, g_decode]
    if not need_input:
        return grads, d_wave, None
    channels = d_pred.shape[0]
    d_nodes = tt(w_encode[:, channels:], d_summed).astype(LOW)
    return grads, d_wave, c_skip * d_pred + c_in * nn(d_nodes, owner_hot)


def exchange_order(rows):
    half = rows.shape[0] // 2
    devices = lax.axis_size("patch")
    up = [(i, (i + 1) % devices) for i in range(devices)]
    down = [(j, i) for i, j in up]
    from_upper = lax.ppermute(rows[:half], "patch", down)
    from_lower = lax.ppermute(rows[half:], "patch", up)
    return jnp.concatenate([from_lower, from_upper], axis=0)


def fill(array, columns):
    return jnp.pad(array, ((0, 0), (0, columns - array.shape[1])))


def pack(encode, project, output, up, noise, decode):
    rows = project.shape[0]
    return jnp.concatenate(
        [project, output, up, fill(encode.T, 256), fill(decode, 128), noise.reshape(rows, -1)], axis=1
    )


def on_device(
    previous_state, target_state, noise_draws, noise_level, pixel_owner, mesh_to_grid, neighbours, halo_send,
    node_count, pixel_count, w_encode, w_project, w_output, w_up, w_down, w_noise, w_decode,
    m_encode, m_project, m_output, m_up, m_down, m_noise, m_decode,
    v_encode, v_project, v_output, v_up, v_down, v_noise, v_decode,
):
    width = w_project.shape[1] // 3
    hidden = w_up.shape[1]
    channels = previous_state.shape[1]
    rows = w_project.shape[0]
    packed = pack(*(w.astype(LOW) for w in (w_encode, w_project, w_output, w_up, w_noise, w_decode)))
    all_wide = lax.all_gather(packed, BOTH, axis=0, tiled=True)
    all_down = lax.all_gather(w_down.astype(LOW), BOTH, axis=0, tiled=True)
    at = [0, 3 * width, 4 * width, 4 * width + hidden, 4 * width + hidden + 256, 4 * width + hidden + 384]
    w_low = (
        all_wide[:, at[3] : at[3] + 2 * channels],
        all_wide[:, : at[1]],
        all_wide[:, at[1] : at[2]],
        all_wide[:, at[2] : at[3]],
        all_down,
        all_wide[:, at[4] : at[4] + channels],
    )
    devices = width // rows
    low_noise = all_wide[:, at[5] :].reshape(devices, FOUR, -1).transpose(1, 0, 2).reshape(FOUR, -1)

    previous, target = previous_state[0], target_state[0]
    noise_now, levels = noise_draws[0], noise_level[0]
    owners, decode_idx, near_idx, send_idx = pixel_owner[0], mesh_to_grid[0], neighbours[0], halo_send[0]
    nodes = near_idx.shape[0]
    halo = send_idx.shape[0] // 2
    pixels = owners.shape[0]
    pixel_live = (jnp.arange(pixels) < pixel_count[0, 0]).astype(WIDE)
    node_col = jnp.arange(nodes)[:, None]
    owner_hot = ((owners[None, :] == node_col) & (pixel_live[None, :] > 0.0)).astype(LOW)
    counted = jnp.maximum(jnp.sum(owner_hot, axis=1, dtype=WIDE), 1.0)[:, None]
    node_hot = sum((decode_idx[i][None, :] == node_col).astype(WIDE) for i in range(3)).astype(LOW)
    place = jnp.arange(nodes + 2 * halo)[None, :]
    listed = sum((near_idx[:, j : j + 1] == place).astype(WIDE) for j in range(1, NEIGH))
    listed = jnp.where((place >= nodes) | (place < node_count[0, 0]), listed, 0.0)
    listed = listed + (near_idx[:, :1] == place).astype(WIDE)
    send_hot = (send_idx[:, None] == jnp.arange(nodes)[None, :]).astype(LOW)
    shared = (owner_hot, counted, node_hot, listed, send_hot)

    waves = [fourier(levels[i]) for i in range(2)]
    modulate = jnp.dot(jnp.stack(waves), low_noise.astype(WIDE), precision=lax.Precision.HIGHEST)
    modulate = modulate.reshape(2, 4, width)
    sums_previous = nt(owner_hot, previous.astype(LOW))
    noisy_one = target + levels[0] * noise_now[0]
    pred_one, kept_one = forward(w_low, modulate[0], noisy_one, levels[0], sums_previous, shared)
    noisy_two = pred_one + levels[1] * noise_now[1]
    pred_two, kept_two = forward(w_low, modulate[1], noisy_two, levels[1], sums_previous, shared)
    error = (pred_two - target) * pixel_live[None, :]
    loss_local = jnp.sum(error * error)
    count_local = channels * jnp.sum(pixel_live)
    grads_two, wave_two, d_noisy = backward(w_low, modulate[1], kept_two, 2.0 * error, shared, True)
    grads_one, wave_one, _ = backward(w_low, modulate[0], kept_one, d_noisy, shared, False)
    g_encode, g_project, g_output, g_up, g_down, g_decode = [a + b for a, b in zip(grads_one, grads_two)]
    g_noise = waves[0][:, None] * wave_one[None, :] + waves[1][:, None] * wave_two[None, :]
    g_noise = g_noise.reshape(FOUR, devices, -1).transpose(1, 0, 2).reshape(width, -1)
    g_wide = jnp.concatenate(
        [g_project, g_output, g_up, fill(g_encode, 256), fill(g_decode, 128), g_noise], axis=1
    )
    s_wide = lax.psum_scatter(g_wide.astype(LOW), BOTH, scatter_dimension=0, tiled=True).astype(WIDE)
    s_down = lax.psum_scatter(g_down.astype(LOW), BOTH, scatter_dimension=0, tiled=True).astype(WIDE)
    shards = (
        s_wide[:, at[3] : at[3] + 2 * channels].T,
        s_wide[:, : at[1]],
        s_wide[:, at[1] : at[2]],
        s_wide[:, at[2] : at[3]],
        s_down,
        s_wide[:, at[5] :].reshape(FOUR, -1),
        s_wide[:, at[4] : at[4] + channels],
    )
    squares = jnp.sum(s_wide * s_wide) + jnp.sum(s_down * s_down)
    totals = lax.psum((squares, loss_local, count_local), BOTH)
    grad_norm = jnp.sqrt(totals[0])
    factor = THRESHOLD / jnp.maximum(grad_norm, THRESHOLD)
    masters = (w_encode, w_project, w_output, w_up, w_down, w_noise, w_decode)
    moments = (m_encode, m_project, m_output, m_up, m_down, m_noise, m_decode)
    seconds = (v_encode, v_project, v_output, v_up, v_down, v_noise, v_decode)
    new_weights, new_moments, new_seconds = ([], [], [])
    for w, m, v, g in zip(masters, moments, seconds, shards):
        clipped = g * factor
        moment = BETA_ONE * m + (1.0 - BETA_ONE) * clipped
        variance = BETA_TWO * v + (1.0 - BETA_TWO) * clipped * clipped
        stepped = (
            moment
            / (1.0 - BETA_ONE**STEP)
            / (jnp.sqrt(variance / (1.0 - BETA_TWO**STEP)) + EPSILON)
        )
        new_weights.append(w - LEARN_RATE * (stepped + DECAY_RATE * w))
        new_moments.append(moment)
        new_seconds.append(variance)
    return (
        tuple(new_weights)
        + tuple(new_moments)
        + tuple(new_seconds)
        + (totals[1], totals[2], grad_norm)
    )


def solution(mesh):
    in_specs = (
        P("rep", None, "patch"),
        P("rep", None, "patch"),
        P("rep", None, None, "patch"),
        P("rep", None),
        P("rep", "patch"),
        P("rep", None, "patch"),
        P("rep", "patch", None),
        P("rep", "patch"),
        P("rep", "patch"),
        P("rep", "patch"),
        P(None, ("patch", "rep")),
        P(("patch", "rep"), None),
        P(("patch", "rep"), None),
        P(("patch", "rep"), None),
        P(("patch", "rep"), None),
        P(None, ("patch", "rep")),
        P(("patch", "rep"), None),
        P(None, ("patch", "rep")),
        P(("patch", "rep"), None),
        P(("patch", "rep"), None),
        P(("patch", "rep"), None),
        P(("patch", "rep"), None),
        P(None, ("patch", "rep")),
        P(("patch", "rep"), None),
        P(None, ("patch", "rep")),
        P(("patch", "rep"), None),
        P(("patch", "rep"), None),
        P(("patch", "rep"), None),
        P(("patch", "rep"), None),
        P(None, ("patch", "rep")),
        P(("patch", "rep"), None),
    )
    out_specs = (
        P(None, ("patch", "rep")),
        P(("patch", "rep"), None),
        P(("patch", "rep"), None),
        P(("patch", "rep"), None),
        P(("patch", "rep"), None),
        P(None, ("patch", "rep")),
        P(("patch", "rep"), None),
        P(None, ("patch", "rep")),
        P(("patch", "rep"), None),
        P(("patch", "rep"), None),
        P(("patch", "rep"), None),
        P(("patch", "rep"), None),
        P(None, ("patch", "rep")),
        P(("patch", "rep"), None),
        P(None, ("patch", "rep")),
        P(("patch", "rep"), None),
        P(("patch", "rep"), None),
        P(("patch", "rep"), None),
        P(("patch", "rep"), None),
        P(None, ("patch", "rep")),
        P(("patch", "rep"), None),
        P(),
        P(),
        P(),
    )
    return jax.shard_map(
        on_device, mesh=mesh, in_specs=in_specs, out_specs=out_specs, check_vma=False
    )
```

time: 2120 us -> 674 us (0.32)
  waiting for transfers between devices: 829 us -> 237 us
  local copies, waits for them, and re-layouts: 418 us -> 51 us
  other arithmetic: 471 us -> 127 us
  blocking collectives: 201 us -> 40.3 us
  matrix products: 139 us -> 161 us
    reduce_scatter x6 -> x2, waiting for transfers between devices: 697 us -> 175 us  [the longest x1 108 us: on_device(): lax.psum_scatter(g_wide.astype(LOW), BOTH, scatter_dimension=0, tiled=True)]
    scatter-add x12 -> x0, other arithmetic: 278 us -> none  [the longest x2 145 us: backward(): dextended = jnp.zeros(extended.shape, jnp.float32).at[near_idx].add(d_near)]
    gather x12 -> x0, local copies, waits for them, and re-layouts: 199 us -> none  [the longest x2 71.2 us: split_near(): near = extended[near_idx]]
    all_gather x4 -> x0, blocking collectives: 164 us -> none  [the longest x1 44.2 us: on_device(): lax.all_gather(low_encode, ('patch', 'rep'), axis=1, tiled=True)]
    unnamed x11 -> x4, waiting for transfers between devices: 132 us -> 0.07 us
    reshape x10 -> x4, local copies, waits for them, and re-layouts: 109 us -> 0.6 us  [the longest x3 0.51 us: on_device(): all_wide[:, at[5]:].reshape(devices, FOUR, -1).transpose(1, 0, 2)]
    concatenate x6 -> x4, other arithmetic: 49.4 us -> 0.2 us  [the longest x2 0.19 us: forward(): jnp.concatenate([keyval, exchange(nn(send_hot, keyval).astype(LOW))], axi...]
    unnamed x3 -> x5, other arithmetic: 49.1 us -> 2.57 us
  transfers between devices with their start and end apart: 18 -> 12, of which waited for: 7 -> 8; matrix products, arithmetic and copies ran while one was open for 12% -> 19% of each run, Pallas kernels for 0% -> 0%
where the time goes in v1:
time: 674 us; the launch traced here: 664 us
  waiting for transfers between devices  237 us (35%)
  matrix products  161 us (24%)
  other arithmetic  127 us (19%)
  local copies, waits for them, and re-layouts  51 us (8%)
  blocking collectives  40.3 us (6%)
  between operations  27.5 us (4%)
  starting transfers between devices  19.8 us (3%)
    reduce_scatter x1, waiting for transfers between devices, on_device(): lax.psum_scatter(g_wide.astype(LOW), BOTH, scatter_dimension=0, tiled=True)  108 us
    dot_general x33, matrix products, nt(): lax.dot_general(a, b, (((1,), (1,)), ((), ())), preferred_element_type=WIDE)  69.9 us
    reduce_scatter x1, waiting for transfers between devices, on_device(): lax.psum_scatter(g_down.astype(LOW), BOTH, scatter_dimension=0, tiled=True)  66.8 us
    dot_general x29, matrix products, nn(): lax.dot_general(a, b, (((1,), (0,)), ((), ())), preferred_element_type=WIDE)  52.3 us
    all_gather x1, waiting for transfers between devices, on_device(): all_wide = lax.all_gather(packed, BOTH, axis=0, tiled=True)  46.1 us
    psum x1, blocking collectives, on_device(): totals = lax.psum((squares, loss_local, count_local), BOTH)  40.3 us
    dot_general x30, matrix products, tn(): lax.dot_general(a, b, (((0,), (0,)), ((), ())), preferred_element_type=WIDE)  39.2 us
    convert_element_type x8, other arithmetic, backward(): d_low = (d_scores * SCALE).astype(LOW)  30.5 us
  transfers between devices with their start and end apart: 12, of which 8 were waited for; matrix products, arithmetic and copies ran while one was open for 19% of the time, Pallas kernels for 0%

profile of v1, /device:TPU:0, one launch (start us, length us, event | category | flops | bytes accessed | tf_op | source)
XLA Modules:
  0.0 663.9 jit_solution(2018250951772266)
XLA Ops:
  33.3 46.1 %all-gather.3.cloned.1.call-done = bf16[512,4608]{1,0:T(8,128)(2,1)} async-done(((bf16[16,4608]{1,0:T(8,128)(2,1)}), bf16[512,4608]{1,0:T(8,128)(2,1)}) %all-gather.3.cloned.1.call-update) | async-done | bytes 4718608 | tf_op jit(solution)/shard_map/all_gather | solution.py:206
  87.8 3.4 collective-permute-start.1
  102.7 3.5 fusion.226
  106.3 3.7 broadcast_divide_fusion.4
  110.4 3.5 fusion.225
  114.0 3.7 broadcast_divide_fusion.5
  120.2 3.5 fusion.224
  123.8 3.7 broadcast_divide_fusion.6
  127.9 3.5 fusion.223
  131.5 4.2 broadcast_divide_fusion.7
  138.1 3.4 fusion.58
  141.5 4.5 fusion.60
  146.1 6.8 %fusion.11 = f32[84,3072]{1,0:T(8,128)} fusion(s32[3072]{0:T(1024)S(1)} %bitcast.550, s32[3072]{0:T(1024)S(1)} %bitcast.554, s32[3072]{0:T(1024)S(1)} %bitcast.544, bf16[512,512]{0,1:T(8,128)(2,1)S(1)} %fusion.60, f32[1,1,84,3072]{3,1,2,0:T(1,128)S(1)} %copy-done.90, f32[]{:T(128)} %bitcast.6, f32[]{:T(128)S(6)} %mul.829, f32[]{:T(128)S(6)} %div.267, ...), kind=kOutput, calls=%fused_computation.23 | convolution fusion | flops 324286464 | bytes 4822024 | tf_op jit(solution)/shard_map/dot_general | solution.py:27
  161.2 4.7 collective-permute-start.3
  171.2 3.7 fusion.230
  174.9 3.7 broadcast_divide_fusion
  179.1 3.5 fusion.229
  182.6 3.7 broadcast_divide_fusion.1
  186.8 3.5 fusion.227
  190.4 3.7 broadcast_divide_fusion.3
  194.5 3.5 fusion.228
  198.1 3.9 broadcast_divide_fusion.2
  209.1 6.2 multiply_reduce_fusion.8
  215.3 3.5 fusion.75
  224.2 5.1 multiply_convert_fusion.1
  229.3 5.2 fusion.302
  249.5 3.5 multiply_convert_fusion.11
  257.7 6.1 multiply_convert_fusion.10
  267.2 3.5 multiply_convert_fusion.9
  273.1 3.5 multiply_convert_fusion.8
  281.6 4.6 collective-permute-start.5
  287.4 4.6 collective-permute-done.4
  295.2 3.6 fusion.303
  305.2 4.1 fusion.24
  309.4 3.4 fusion.74
  321.9 5.1 multiply_convert_fusion
  330.4 4.6 fusion.304
  349.9 3.5 multiply_convert_fusion.7
  362.2 3.5 multiply_convert_fusion.6
  369.1 3.5 multiply_convert_fusion.5
  375.9 3.5 multiply_convert_fusion.4
  388.0 4.9 collective-permute-start.7
  394.8 4.2 collective-permute-done.6
  398.9 3.6 collective-permute-done.7
  406.0 3.4 fusion.305
  429.7 66.8 %reduce-scatter.5.cloned.1.call-done = bf16[64,512]{1,0:T(8,128)(2,1)} async-done(((bf16[2048,512]{1,0:T(8,128)(2,1)}), bf16[64,512]{1,0:T(8,128)(2,1)}) %reduce-scatter.5.cloned.1.call-update) | async-done | bytes 65552 | tf_op jit(solution)/shard_map/reduce_scatter | solution.py:258
  498.0 107.8 %reduce-scatter.3.cloned.1.call-done = bf16[16,4608]{1,0:T(8,128)(2,1)} async-done(((bf16[512,4608]{1,0:T(8,128)(2,1)}), bf16[16,4608]{1,0:T(8,128)(2,1)}) %reduce-scatter.3.cloned.1.call-update) | async-done | bytes 147472 | tf_op jit(solution)/shard_map/reduce_scatter | solution.py:257
  608.7 40.3 %all-reduce.4 = (f32[]{:T(128)}, f32[]{:T(128)}, f32[]{:T(128)}) all-reduce(f32[]{:T(128)S(6)} %add.436, f32[]{:T(128)} %get-tuple-element.147, f32[]{:T(128)S(6)} %mul_shard_map.3), channel_id=1, replica_groups=mesh['patch'=8,'rep'=4] {'patch','rep'}, use_global_device_ids=true, to_apply=%region_53.54 | all-reduce | flops 3 | bytes 24 | tf_op jit(solution)/shard_map/psum | solution.py:269
  (620 shorter events, 196.9 us)
Async XLA Ops:
  7.2 72.2 %all-gather.3.cloned.1.call-start = ((), (), s32[]{:S(2)}) async-start(), calls=%async_computation.2 | async-start | bytes 4866048 | tf_op jit(solution)/shard_map/all_gather | solution.py:206
  12.9 128.7 %all-gather.5.cloned.1.call-start = ((), (), s32[]{:S(2)}) async-start(), calls=%async_computation.3 | async-start | bytes 2162688 | tf_op jit(solution)/shard_map/all_gather | solution.py:207
  14.5 482.0 %reduce-scatter.5.cloned.1.call-start = ((), (), s32[]{:S(2)}) async-start(), calls=%async_computation.5 | async-start | bytes 2162688 | tf_op jit(solution)/shard_map/reduce_scatter | solution.py:258
  20.6 132.3 %copy-start.177 = (pred[3072]{0:T(1024)(128)(4,1)}, pred[3072]{0:T(1024)(128)(4,1)S(1)}, u32[]{:S(2)}) copy-start(pred[3072]{0:T(1024)(128)(4,1)S(1)} %get-tuple-element.150) | copy-start | bytes 9220
  22.5 133.2 %copy-start.170 = (f32[512]{0:T(512)}, f32[512]{0:T(512)S(1)}, u32[]{:S(2)}) copy-start(f32[512]{0:T(512)S(1)} %broadcast_maximum_fusion) | copy-start | bytes 6148
  25.0 121.1 %copy-start.160 = (s32[1,1,3072]{2,0,1:T(1,128)}, s32[1,1,3072]{2,0,1:T(1,128)S(1)}, u32[]{:S(2)}) copy-start(s32[1,1,3072]{2,0,1:T(1,128)S(1)} %get-tuple-element.70) | copy-start | bytes 36868
  27.3 54.3 %copy-start.122 = (bf16[512,84]{0,1:T(8,128)(2,1)}, bf16[512,84]{0,1:T(8,128)(2,1)S(1)}, u32[]{:S(2)}) copy-start(bf16[512,84]{0,1:T(8,128)(2,1)S(1)} %fusion.77) | copy-start | bytes 258052
  33.3 49.6 %copy-start.201 = (bf16[512,84]{0,1:T(8,128)(2,1)}, bf16[512,84]{0,1:T(8,128)(2,1)S(1)}, u32[]{:S(2)}) copy-start(bf16[512,84]{0,1:T(8,128)(2,1)S(1)} %fusion.80) | copy-start | bytes 258052
  81.6 75.6 %copy-start.166 = (f32[1,512]{1,0:T(1,128)}, f32[1,512]{1,0:T(1,128)S(1)}, u32[]{:S(2)}) copy-start(f32[1,512]{1,0:T(1,128)S(1)} %get-tuple-element.91) | copy-start | bytes 6148
  82.9 54.3 %copy-start.51 = (f32[512,512]{0,1:T(8,128)}, f32[512,512]{0,1:T(8,128)S(1)}, u32[]{:S(2)}) copy-start(f32[512,512]{0,1:T(8,128)S(1)} %get-tuple-element.100) | copy-start | bytes 3145732
  86.2 11.7 %collective-permute-start = (bf16[64,1024]{1,0:T(8,128)(2,1)S(1)}, bf16[64,1024]{1,0:T(8,128)(2,1)S(1)}, u32[]{:S(2)}, u32[]{:S(2)}) collective-permute-start(bf16[64,1024]{1,0:T(8,128)(2,1)S(1)} %get-tuple-element.68), channel_id=1, source_target_pairs={{0,4},{4,8},{8,12},{12,16},{16,20},{20,24},{24,28},{28,0},{1,5},{5... | collective-permute-start | bytes 393224 | tf_op jit(solution)/shard_map/ppermute | solution.py:69
  87.8 10.2 %collective-permute-start.1 = (bf16[64,1024]{1,0:T(8,128)(2,1)S(1)}, bf16[64,1024]{1,0:T(8,128)(2,1)S(1)}, u32[]{:S(2)}, u32[]{:S(2)}) collective-permute-start(bf16[64,1024]{1,0:T(8,128)(2,1)S(1)} %get-tuple-element.69), channel_id=1, source_target_pairs={{4,0},{8,4},{12,8},{16,12},{20,16},{24,20},{28,24},{0,28},{5,1},{9... | collective-permute-start | bytes 393224 | tf_op jit(solution)/shard_map/ppermute | solution.py:70
  98.0 37.7 %copy-start.44 = (bf16[640,1024]{1,0:T(8,128)(2,1)}, bf16[640,1024]{1,0:T(8,128)(2,1)S(1)}, u32[]{:S(2)}) copy-start(bf16[640,1024]{1,0:T(8,128)(2,1)S(1)} %pad_maximum_fusion) | copy-start | bytes 3932164
  102.7 21.1 %copy-start.15 = (f32[512,640]{1,0:T(8,128)}, f32[512,640]{1,0:T(8,128)S(1)}, u32[]{:S(2)}) copy-start(f32[512,640]{1,0:T(8,128)S(1)} %get-tuple-element.108) | copy-start | bytes 3932164
  110.4 26.8 %copy-start.93 = (bf16[512,128]{0,1:T(8,128)(2,1)}, bf16[512,128]{0,1:T(8,128)(2,1)S(1)}, u32[]{:S(2)}) copy-start(bf16[512,128]{0,1:T(8,128)(2,1)S(1)} %convolution_convert_fusion.18) | copy-start | bytes 393220
  117.7 19.5 %slice-start = ((s8[4718592]{0:T(1024)(128)(4,1)}), s8[4194304]{0:T(1024)(128)(4,1)S(1)}, s32[]{:S(2)}) async-start(s8[4718592]{0:T(1024)(128)(4,1)} %bitcast.118), calls=%async_computation.6 | async-start | bytes 8388608
  161.2 7.9 %collective-permute-start.2 = (bf16[64,1024]{1,0:T(8,128)(2,1)S(1)}, bf16[64,1024]{1,0:T(8,128)(2,1)S(1)}, u32[]{:S(2)}, u32[]{:S(2)}) collective-permute-start(bf16[64,1024]{1,0:T(8,128)(2,1)S(1)} %get-tuple-element.66), channel_id=1, source_target_pairs={{0,4},{4,8},{8,12},{12,16},{16,20},{20,24},{24,28},{28,0},{1,5},{5... | collective-permute-start | bytes 393224 | tf_op jit(solution)/shard_map/ppermute | solution.py:69
  161.2 7.9 %collective-permute-start.3 = (bf16[64,1024]{1,0:T(8,128)(2,1)S(1)}, bf16[64,1024]{1,0:T(8,128)(2,1)S(1)}, u32[]{:S(2)}, u32[]{:S(2)}) collective-permute-start(bf16[64,1024]{1,0:T(8,128)(2,1)S(1)} %get-tuple-element.67), channel_id=1, source_target_pairs={{4,0},{8,4},{12,8},{16,12},{20,16},{24,20},{28,24},{0,28},{5,1},{9... | collective-permute-start | bytes 393224 | tf_op jit(solution)/shard_map/ppermute | solution.py:70
  169.2 32.7 %copy-start.46 = (bf16[640,1024]{1,0:T(8,128)(2,1)}, bf16[640,1024]{1,0:T(8,128)(2,1)S(1)}, u32[]{:S(2)}) copy-start(bf16[640,1024]{1,0:T(8,128)(2,1)S(1)} %pad_maximum_fusion.1) | copy-start | bytes 3932164
  179.1 24.4 %copy-start.101 = (bf16[512,128]{0,1:T(8,128)(2,1)}, bf16[512,128]{0,1:T(8,128)(2,1)S(1)}, u32[]{:S(2)}) copy-start(bf16[512,128]{0,1:T(8,128)(2,1)S(1)} %convolution_convert_fusion.14) | copy-start | bytes 393220
  182.6 20.8 %slice-start.2 = ((s8[4718592]{0:T(1024)(128)(4,1)}), s8[4194304]{0:T(1024)(128)(4,1)S(1)}, s32[]{:S(2)}) async-start(s8[4718592]{0:T(1024)(128)(4,1)} %bitcast.120), calls=%async_computation.8 | async-start | bytes 8388608
  281.2 10.8 %collective-permute-start.4 = (bf16[64,1024]{0,1:T(8,128)(2,1)S(1)}, bf16[64,1024]{0,1:T(8,128)(2,1)S(1)}, u32[]{:S(2)}, u32[]{:S(2)}) collective-permute-start(bf16[64,1024]{0,1:T(8,128)(2,1)S(1)} %get-tuple-element.64), channel_id=1, source_target_pairs={{0,4},{4,8},{8,12},{12,16},{16,20},{20,24},{24,28},{28,0},{1,5},{5... | collective-permute-start | bytes 393224 | tf_op jit(solution)/shard_map/ppermute | solution.py:180
  281.6 13.1 %collective-permute-start.5 = (bf16[64,1024]{0,1:T(8,128)(2,1)S(1)}, bf16[64,1024]{0,1:T(8,128)(2,1)S(1)}, u32[]{:S(2)}, u32[]{:S(2)}) collective-permute-start(bf16[64,1024]{0,1:T(8,128)(2,1)S(1)} %get-tuple-element.65), channel_id=1, source_target_pairs={{4,0},{8,4},{12,8},{16,12},{20,16},{24,20},{28,24},{0,28},{5,1},{9... | collective-permute-start | bytes 393224 | tf_op jit(solution)/shard_map/ppermute | solution.py:179
  359.2 246.6 %reduce-scatter.3.cloned.1.call-start = ((), (), s32[]{:S(2)}) async-start(), calls=%async_computation.4 | async-start | bytes 4866048 | tf_op jit(solution)/shard_map/reduce_scatter | solution.py:257
  387.9 11.0 %collective-permute-start.6 = (bf16[64,1024]{0,1:T(8,128)(2,1)}, bf16[64,1024]{0,1:T(8,128)(2,1)}, u32[]{:S(2)}, u32[]{:S(2)}) collective-permute-start(bf16[64,1024]{0,1:T(8,128)(2,1)} %get-tuple-element.62), channel_id=1, source_target_pairs={{0,4},{4,8},{8,12},{12,16},{16,20},{20,24},{24,28},{28,0},{1,5},{5... | collective-permute-start | bytes 393224 | tf_op jit(solution)/shard_map/ppermute | solution.py:180
  388.0 14.5 %collective-permute-start.7 = (bf16[64,1024]{0,1:T(8,128)(2,1)}, bf16[64,1024]{0,1:T(8,128)(2,1)}, u32[]{:S(2)}, u32[]{:S(2)}) collective-permute-start(bf16[64,1024]{0,1:T(8,128)(2,1)} %get-tuple-element.63), channel_id=1, source_target_pairs={{4,0},{8,4},{12,8},{16,12},{20,16},{24,20},{28,24},{0,28},{5,1},{9... | collective-permute-start | bytes 393224 | tf_op jit(solution)/shard_map/ppermute | solution.py:179
  428.2 222.5 %copy-start.131 = (f32[16,84]{1,0:T(8,128)S(1)}, f32[16,84]{1,0:T(8,128)}, u32[]{:S(2)}) copy-start(f32[16,84]{1,0:T(8,128)} %param.47) | copy-start | bytes 16132
  428.2 222.5 %copy-start.172 = (f32[16,84]{1,0:T(8,128)S(1)}, f32[16,84]{1,0:T(8,128)}, u32[]{:S(2)}) copy-start(f32[16,84]{1,0:T(8,128)} %param.54) | copy-start | bytes 16132
  428.2 222.5 %copy-start.173 = (f32[16,84]{1,0:T(8,128)S(1)}, f32[16,84]{1,0:T(8,128)}, u32[]{:S(2)}) copy-start(f32[16,84]{1,0:T(8,128)} %param.61) | copy-start | bytes 16132
  428.2 223.2 %copy-start.127 = (f32[168,16]{0,1:T(8,128)S(1)}, f32[168,16]{0,1:T(8,128)}, u32[]{:S(2)}) copy-start(f32[168,16]{0,1:T(8,128)} %param.41) | copy-start | bytes 32260
  428.2 223.2 %copy-start.154 = (f32[168,16]{0,1:T(8,128)S(1)}, f32[168,16]{0,1:T(8,128)}, u32[]{:S(2)}) copy-start(f32[168,16]{0,1:T(8,128)} %param.48) | copy-start | bytes 32260
  428.3 223.2 %copy-start.155 = (f32[168,16]{0,1:T(8,128)S(1)}, f32[168,16]{0,1:T(8,128)}, u32[]{:S(2)}) copy-start(f32[168,16]{0,1:T(8,128)} %param.55) | copy-start | bytes 32260
  428.3 223.8 %copy-start.117 = (f32[16,512]{1,0:T(8,128)S(1)}, f32[16,512]{1,0:T(8,128)}, u32[]{:S(2)}) copy-start(f32[16,512]{1,0:T(8,128)} %param.43) | copy-start | bytes 98308
  428.3 223.8 %copy-start.129 = (f32[16,512]{1,0:T(8,128)S(1)}, f32[16,512]{1,0:T(8,128)}, u32[]{:S(2)}) copy-start(f32[16,512]{1,0:T(8,128)} %param.50) | copy-start | bytes 98308
  428.3 223.8 %copy-start.130 = (f32[16,512]{1,0:T(8,128)S(1)}, f32[16,512]{1,0:T(8,128)}, u32[]{:S(2)}) copy-start(f32[16,512]{1,0:T(8,128)} %param.57) | copy-start | bytes 98308
  428.3 224.4 %copy-start.110 = (f32[16,1536]{1,0:T(8,128)S(1)}, f32[16,1536]{1,0:T(8,128)}, u32[]{:S(2)}) copy-start(f32[16,1536]{1,0:T(8,128)} %param.42) | copy-start | bytes 294916
  428.3 224.4 %copy-start.120 = (f32[16,1536]{1,0:T(8,128)S(1)}, f32[16,1536]{1,0:T(8,128)}, u32[]{:S(2)}) copy-start(f32[16,1536]{1,0:T(8,128)} %param.49) | copy-start | bytes 294916
  428.3 224.4 %copy-start.121 = (f32[16,1536]{1,0:T(8,128)S(1)}, f32[16,1536]{1,0:T(8,128)}, u32[]{:S(2)}) copy-start(f32[16,1536]{1,0:T(8,128)} %param.56) | copy-start | bytes 294916
  428.4 225.1 %copy-start.106 = (f32[16,2048]{1,0:T(8,128)S(1)}, f32[16,2048]{1,0:T(8,128)}, u32[]{:S(2)}) copy-start(f32[16,2048]{1,0:T(8,128)} %param.44) | copy-start | bytes 393220
  428.4 225.1 %copy-start.115 = (f32[16,2048]{1,0:T(8,128)S(1)}, f32[16,2048]{1,0:T(8,128)}, u32[]{:S(2)}) copy-start(f32[16,2048]{1,0:T(8,128)} %param.51) | copy-start | bytes 393220
  428.4 225.1 %copy-start.116 = (f32[16,2048]{1,0:T(8,128)S(1)}, f32[16,2048]{1,0:T(8,128)}, u32[]{:S(2)}) copy-start(f32[16,2048]{1,0:T(8,128)} %param.58) | copy-start | bytes 393220
  497.9 156.4 %copy-start.128 = (f32[32,64]{1,0:T(8,128)S(1)}, f32[32,64]{1,0:T(8,128)}, u32[]{:S(2)}) copy-start(f32[32,64]{1,0:T(8,128)} %param.46) | copy-start | bytes 24580
  497.9 156.4 %copy-start.156 = (f32[32,64]{1,0:T(8,128)S(1)}, f32[32,64]{1,0:T(8,128)}, u32[]{:S(2)}) copy-start(f32[32,64]{1,0:T(8,128)} %param.53) | copy-start | bytes 24580
  497.9 156.4 %copy-start.157 = (f32[32,64]{1,0:T(8,128)S(1)}, f32[32,64]{1,0:T(8,128)}, u32[]{:S(2)}) copy-start(f32[32,64]{1,0:T(8,128)} %param.60) | copy-start | bytes 24580
  607.4 47.6 %copy-start.109 = (f32[64,512]{1,0:T(8,128)S(1)}, f32[64,512]{1,0:T(8,128)}, u32[]{:S(2)}) copy-start(f32[64,512]{1,0:T(8,128)} %param.45) | copy-start | bytes 393220
  607.4 47.6 %copy-start.113 = (bf16[64,512]{1,0:T(8,128)(2,1)S(1)}, bf16[64,512]{1,0:T(8,128)(2,1)}, u32[]{:S(2)}) copy-start(bf16[64,512]{1,0:T(8,128)(2,1)} %reduce-scatter.5.cloned.1.call-done) | copy-start | bytes 196612
  607.4 47.6 %copy-start.118 = (f32[64,512]{1,0:T(8,128)S(1)}, f32[64,512]{1,0:T(8,128)}, u32[]{:S(2)}) copy-start(f32[64,512]{1,0:T(8,128)} %param.52) | copy-start | bytes 393220
  607.4 47.6 %copy-start.119 = (f32[64,512]{1,0:T(8,128)S(1)}, f32[64,512]{1,0:T(8,128)}, u32[]{:S(2)}) copy-start(f32[64,512]{1,0:T(8,128)} %param.59) | copy-start | bytes 393220
  (171 other events, 769.4 us)
Sparse Core Ops, SparseCore 0:
  13.0 66.3 all-gather.2
  82.8 56.7 all-gather.4
  359.3 137.0 reduce-scatter.4
  502.7 103.0 reduce-scatter.2

commit v2 on v1

--- a/solution.py
+++ b/solution.py
@@ -1,6 +1,8 @@
 import jax
 import jax.numpy as jnp
 from jax import lax
+from jax.experimental import pallas as pl
+from jax.experimental.pallas import tpu as pltpu
 from jax.sharding import PartitionSpec as P
 
 HEADS = 4
@@ -21,6 +23,207 @@
 LOW = jnp.bfloat16
 WIDE = jnp.float32
 SCALE = HD ** (-0.5)
+
+
+MESH = pl.DeviceIdType.MESH
+GRID = (4, 2, 2, 2)
+
+
+def places():
+    patch, rep = lax.axis_index("patch"), lax.axis_index("rep")
+    z, y, x, c = patch // 2, patch % 2, rep // 2, rep % 2
+    sibling = {"patch": patch, "rep": x * 2 + (1 - c)}
+    across_x = {"patch": patch, "rep": (1 - x) * 2 + c}
+    across_y = {"patch": z * 2 + (1 - y), "rep": rep}
+    along_z = [{"patch": ((z + d) % 4) * 2 + y, "rep": rep} for d in range(4)]
+    return z, y, x, c, sibling, across_x, across_y, along_z
+
+
+def greet(others):
+    barrier = pltpu.get_barrier_semaphore()
+    for other in others:
+        pl.semaphore_signal(barrier, inc=1, device_id=other, device_id_type=MESH)
+    pl.semaphore_wait(barrier, len(others))
+
+
+def send(src, dst, sems, index, device):
+    copy = pltpu.make_async_remote_copy(
+        src_ref=src, dst_ref=dst, send_sem=sems.at[(0,) + index], recv_sem=sems.at[(1,) + index],
+        device_id=device, device_id_type=MESH,
+    )
+    copy.start()
+    return copy
+
+
+def plus(*terms):
+    total = terms[0].astype(WIDE)
+    for term in terms[1:]:
+        total = total + term.astype(WIDE)
+    return total
+
+
+def scatter_scratch(rows, cols):
+    h = cols // 2
+    return [
+        pltpu.VMEM((4, 2, 2, rows, cols), LOW),
+        pltpu.VMEM((4, 2, 2, rows, cols), LOW),
+        pltpu.VMEM((4, 2, rows, h), LOW),
+        pltpu.VMEM((4, 2, rows, h), LOW),
+        pltpu.VMEM((4, rows, h), LOW),
+        pltpu.VMEM((4, 2, rows, h), LOW),
+        pltpu.VMEM((4, 2, rows, h), LOW),
+        pltpu.VMEM((4, rows, h), LOW),
+        pltpu.VMEM((3, rows, cols), LOW),
+        pltpu.VMEM((3, rows, cols), LOW),
+    ]
+
+
+def scatter_kernel(g_one, g_two, extra, out_one, out_two, totals, *scratch):
+    z, y, x, c, sibling, across_x, across_y, along_z = places()
+    parts = ((g_one, out_one) + scratch[:10], (g_two, out_two) + scratch[10:20])
+    board, sems, small = scratch[20:]
+    greet([sibling, across_x, across_y] + along_z[1:])
+    steps = [(d, (z + d) % 4) for d in (1, 2, 3, 0)]
+    sent, first, left, right, left_two, right_two, last = [], {}, {}, {}, {}, {}, {}
+    for d, zd in steps:
+        for i, (g, out, near, acc, near_l, acc_l, end_l, near_r, acc_r, end_r, going, come) in enumerate(parts):
+            first[d, i] = send(g.at[zd, :, :, 1 - c], near.at[zd], sems, (0, d, i), sibling)
+    for d, zd in steps:
+        for i, (g, out, near, acc, near_l, acc_l, end_l, near_r, acc_r, end_r, going, come) in enumerate(parts):
+            h = g.shape[-1] // 2
+            first[d, i].wait_recv()
+            acc[zd] = plus(g[zd, :, :, c], near[zd]).astype(LOW)
+            left[d, i] = send(acc.at[zd, :, 1 - x, :, :h], near_l.at[zd], sems, (1, d, i), across_x)
+            right[d, i] = send(acc.at[zd, 1 - y, :, :, h:], near_r.at[zd], sems, (2, d, i), across_y)
+    for d, zd in steps:
+        for i, (g, out, near, acc, near_l, acc_l, end_l, near_r, acc_r, end_r, going, come) in enumerate(parts):
+            h = g.shape[-1] // 2
+            left[d, i].wait_recv()
+            acc_l[zd] = plus(acc[zd, :, x, :, :h], near_l[zd]).astype(LOW)
+            left_two[d, i] = send(acc_l.at[zd, 1 - y], end_l.at[zd], sems, (3, d, i), across_y)
+            right[d, i].wait_recv()
+            acc_r[zd] = plus(acc[zd, y, :, :, h:], near_r[zd]).astype(LOW)
+            right_two[d, i] = send(acc_r.at[zd, 1 - x], end_r.at[zd], sems, (4, d, i), across_x)
+    for d, zd in steps:
+        for i, (g, out, near, acc, near_l, acc_l, end_l, near_r, acc_r, end_r, going, come) in enumerate(parts):
+            h = g.shape[-1] // 2
+            left_two[d, i].wait_recv()
+            done_l = plus(acc_l[zd, y], end_l[zd])
+            right_two[d, i].wait_recv()
+            done_r = plus(acc_r[zd, x], end_r[zd])
+            if d == 0:
+                out[:, :h] = done_l
+                out[:, h:] = done_r
+            else:
+                going[d - 1, :, :h] = done_l.astype(LOW)
+                going[d - 1, :, h:] = done_r.astype(LOW)
+                last[d, i] = send(going.at[d - 1], come.at[d - 1], sems, (5, d, i), along_z[d])
+    squares = jnp.zeros((), WIDE)
+    for i, part in enumerate(parts):
+        out, come = part[1], part[11]
+        for d in (1, 2, 3):
+            last[d, i].wait_recv()
+        out[...] = plus(out[...], come[0], come[1], come[2])
+        squares = squares + jnp.sum(out[...] * out[...])
+    row = lax.broadcasted_iota(jnp.int32, extra.shape, 0)
+    board[0] = jnp.where(row == 0, squares, extra[...])
+    more = []
+    for phase, device in enumerate((sibling, across_x, across_y)):
+        copy = send(board.at[phase], board.at[4 + phase], small, (phase,), device)
+        copy.wait_recv()
+        more.append(copy)
+        board[phase + 1] = board[phase] + board[4 + phase]
+    for d in (1, 2, 3):
+        more.append(send(board.at[3], board.at[8 + z], small, (2 + d,), along_z[d]))
+    board[8 + z] = board[3]
+    for d in (1, 2, 3):
+        more[2 + d].wait_recv()
+    totals[...] = board[8] + board[9] + board[10] + board[11]
+    for group in (first, left, right, left_two, right_two, last):
+        for copy in group.values():
+            copy.wait_send()
+    for copy in more:
+        copy.wait_send()
+
+
+def reduce_scatter(g_one, g_two, extra):
+    rows = [g.shape[0] // 32 for g in (g_one, g_two)]
+    cols = [g.shape[1] for g in (g_one, g_two)]
+    vmem = pl.BlockSpec(memory_space=pltpu.VMEM)
+    return pl.pallas_call(
+        scatter_kernel,
+        out_shape=[jax.ShapeDtypeStruct((r, n), WIDE) for r, n in zip(rows, cols)]
+        + [jax.ShapeDtypeStruct(extra.shape, WIDE)],
+        in_specs=[vmem] * 3,
+        out_specs=[vmem] * 3,
+        scratch_shapes=scatter_scratch(rows[0], cols[0]) + scatter_scratch(rows[1], cols[1])
+        + [pltpu.VMEM((12,) + extra.shape, WIDE), pltpu.SemaphoreType.DMA((2, 6, 4, 2)),
+           pltpu.SemaphoreType.DMA((2, 6))],
+        compiler_params=pltpu.CompilerParams(
+            collective_id=1, has_side_effects=True, vmem_limit_bytes=48 * 2**20),
+    )(g_one.reshape(GRID + (rows[0], cols[0])), g_two.reshape(GRID + (rows[1], cols[1])), extra)
+
+
+def gather_kernel(a_one, a_two, out_one, out_two, sems, local):
+    z, y, x, c, sibling, across_x, across_y, along_z = places()
+    greet([sibling, across_x, across_y] + along_z[1:])
+    parts = ((a_one, out_one), (a_two, out_two))
+    steps = [(d, (z + d) % 4) for d in (0, 1, 2, 3)]
+    copies, own, x_one, y_one, x_two, y_two, core = [], [], {}, {}, {}, {}, {}
+    planes = {}
+    for i, (a, out) in enumerate(parts):
+        copy = pltpu.make_async_copy(a, out.at[z, y, x, c], local.at[i])
+        copy.start()
+        own.append(copy)
+        for d in (2, 1, 3):
+            planes[d, i] = send(a, out.at[z, y, x, c], sems, (0, d, i), along_z[d])
+    for i in range(2):
+        own[i].wait()
+    for d in range(4):
+        zd = (z - d + 4) % 4
+        for i, (a, out) in enumerate(parts):
+            h = a.shape[-1] // 2
+            if d:
+                planes[d, i].wait_recv()
+            here_l, here_r = out.at[zd, y, x, c, :, :h], out.at[zd, y, x, c, :, h:]
+            x_one[d, i] = send(here_l, here_l, sems, (1, d, i), across_x)
+            y_one[d, i] = send(here_r, here_r, sems, (2, d, i), across_y)
+    for d in range(4):
+        zd = (z - d + 4) % 4
+        for i, (a, out) in enumerate(parts):
+            h = a.shape[-1] // 2
+            x_one[d, i].wait_recv()
+            both = out.at[zd, y, :, c, :, :h]
+            y_two[d, i] = send(both, both, sems, (3, d, i), across_y)
+            y_one[d, i].wait_recv()
+            both = out.at[zd, :, x, c, :, h:]
+            x_two[d, i] = send(both, both, sems, (4, d, i), across_x)
+    for d in range(4):
+        zd = (z - d + 4) % 4
+        for i, (a, out) in enumerate(parts):
+            y_two[d, i].wait_recv()
+            x_two[d, i].wait_recv()
+            plane = out.at[zd, :, :, c]
+            core[d, i] = send(plane, plane, sems, (5, d, i), sibling)
+    for group in (planes, x_one, y_one, x_two, y_two):
+        for copy in group.values():
+            copy.wait_send()
+    for copy in core.values():
+        copy.wait()
+
+
+def all_gather(a_one, a_two):
+    shapes = [a.shape for a in (a_one, a_two)]
+    outs = pl.pallas_call(
+        gather_kernel,
+        out_shape=[jax.ShapeDtypeStruct(GRID + s, LOW) for s in shapes],
+        in_specs=[pl.BlockSpec(memory_space=pltpu.VMEM)] * 2,
+        out_specs=[pl.BlockSpec(memory_space=pl.ANY)] * 2,
+        scratch_shapes=[pltpu.SemaphoreType.DMA((2, 6, 4, 2)), pltpu.SemaphoreType.DMA((2,))],
+        compiler_params=pltpu.CompilerParams(
+            collective_id=2, has_side_effects=True, vmem_limit_bytes=32 * 2**20),
+    )(a_one, a_two)
+    return [o.reshape(32 * s[0], s[1]) for o, s in zip(outs, shapes)]
 
 
 def nn(a, b):
@@ -203,8 +406,12 @@
     channels = previous_state.shape[1]
     rows = w_project.shape[0]
     packed = pack(*(w.astype(LOW) for w in (w_encode, w_project, w_output, w_up, w_noise, w_decode)))
-    all_wide = lax.all_gather(packed, BOTH, axis=0, tiled=True)
-    all_down = lax.all_gather(w_down.astype(LOW), BOTH, axis=0, tiled=True)
+    small_slice = lax.axis_size("patch") == 8 and lax.axis_size("rep") == 4
+    if small_slice:
+        all_wide, all_down = all_gather(packed, w_down.astype(LOW))
+    else:
+        all_wide = lax.all_gather(packed, BOTH, axis=0, tiled=True)
+        all_down = lax.all_gather(w_down.astype(LOW), BOTH, axis=0, tiled=True)
     at = [0, 3 * width, 4 * width, 4 * width + hidden, 4 * width + hidden + 256, 4 * width + hidden + 384]
     w_low = (
         all_wide[:, at[3] : at[3] + 2 * channels],
@@ -254,8 +461,16 @@
     g_wide = jnp.concatenate(
         [g_project, g_output, g_up, fill(g_encode, 256), fill(g_decode, 128), g_noise], axis=1
     )
-    s_wide = lax.psum_scatter(g_wide.astype(LOW), BOTH, scatter_dimension=0, tiled=True).astype(WIDE)
-    s_down = lax.psum_scatter(g_down.astype(LOW), BOTH, scatter_dimension=0, tiled=True).astype(WIDE)
+    if small_slice:
+        row = lax.broadcasted_iota(jnp.int32, (8, 128), 0)
+        extra = jnp.where(row == 1, loss_local, 0.0) + jnp.where(row == 2, count_local, 0.0)
+        s_wide, s_down, totals = reduce_scatter(g_wide.astype(LOW), g_down.astype(LOW), extra)
+        totals = totals[:3, 0]
+    else:
+        s_wide = lax.psum_scatter(g_wide.astype(LOW), BOTH, scatter_dimension=0, tiled=True).astype(WIDE)
+        s_down = lax.psum_scatter(g_down.astype(LOW), BOTH, scatter_dimension=0, tiled=True).astype(WIDE)
+        squares = jnp.sum(s_wide * s_wide) + jnp.sum(s_down * s_down)
+        totals = lax.psum((squares, loss_local, count_local), BOTH)
     shards = (
         s_wide[:, at[3] : at[3] + 2 * channels].T,
         s_wide[:, : at[1]],
@@ -265,8 +480,6 @@
         s_wide[:, at[5] :].reshape(FOUR, -1),
         s_wide[:, at[4] : at[4] + channels],
     )
-    squares = jnp.sum(s_wide * s_wide) + jnp.sum(s_down * s_down)
-    totals = lax.psum((squares, loss_local, count_local), BOTH)
     grad_norm = jnp.sqrt(totals[0])
     factor = THRESHOLD / jnp.maximum(grad_norm, THRESHOLD)
     masters = (w_encode, w_project, w_output, w_up, w_down, w_noise, w_decode)

time: 674 us -> 499 us (0.74)
  waiting for transfers between devices: 237 us -> 11.4 us
  Pallas kernels: 0 us -> 108 us
  blocking collectives: 40.3 us -> 0 us
  matrix products: 161 us -> 145 us
  between operations: 27.5 us -> 13.1 us
  local copies, waits for them, and re-layouts: 51 us -> 64.4 us
    reduce_scatter x2 -> x0, waiting for transfers between devices: 175 us -> none  [the longest x1 108 us: on_device(): lax.psum_scatter(g_wide.astype(LOW), BOTH, scatter_dimension=0, tiled=True)]
    pallas_call x0 -> x2, Pallas kernels: none -> 108 us  [the longest x1 59.7 us: reduce_scatter(): pl.pallas_call(scatter_kernel, out_shape=[jax.ShapeDtypeStruct((r, n), WI...]
    all_gather x2 -> x0, waiting for transfers between devices: 46.1 us -> none  [the longest x1 46.1 us: on_device(): all_wide = lax.all_gather(packed, BOTH, axis=0, tiled=True)]
    psum x1 -> x0, blocking collectives: 40.3 us -> none  [on_device(): totals = lax.psum((squares, loss_local, count_local), BOTH)]
    dot_general x33, matrix products: 69.9 us -> 60.7 us  [nt(): lax.dot_general(a, b, (((1,), (1,)), ((), ())), preferred_element_type=WIDE)]
    mul x0 -> x8, local copies, waits for them, and re-layouts: none -> 9.18 us  [the longest x4 5.53 us: on_device(): waves[0][:, None] * wave_one[None, :]]
    dot_general x29, matrix products: 52.3 us -> 43.8 us  [nn(): lax.dot_general(a, b, (((1,), (0,)), ((), ())), preferred_element_type=WIDE)]
    unnamed x419 -> x441, local copies, waits for them, and re-layouts: 21.1 us -> 24.7 us
  transfers between devices with their start and end apart: 12 -> 8, of which waited for: 8 -> 4; matrix products, arithmetic and copies ran while one was open for 19% -> 4% of each run, Pallas kernels for 0% -> 0%
where the time goes in v2:
time: 499 us; the launch traced here: 489 us
  matrix products  145 us (29%)
  other arithmetic  128 us (26%)
  Pallas kernels  108 us (22%)
  local copies, waits for them, and re-layouts  64.4 us (13%)
  starting transfers between devices  19.8 us (4%)
  between operations  13.1 us (3%)
  waiting for transfers between devices  11.4 us (2%)
    dot_general x33, matrix products, nt(): lax.dot_general(a, b, (((1,), (1,)), ((), ())), preferred_element_type=WIDE)  60.7 us
    pallas_call x1, Pallas kernels, reduce_scatter(): pl.pallas_call(scatter_kernel, out_shape=[jax.ShapeDtypeStruct((r, n), WI...  59.7 us
    pallas_call x1, Pallas kernels, all_gather(): pl.pallas_call(gather_kernel, out_shape=[jax.ShapeDtypeStruct(GRID + s, L...  47.8 us
    dot_general x29, matrix products, nn(): lax.dot_general(a, b, (((1,), (0,)), ((), ())), preferred_element_type=WIDE)  43.8 us
    dot_general x30, matrix products, tn(): lax.dot_general(a, b, (((0,), (0,)), ((), ())), preferred_element_type=WIDE)  40.5 us
    div x8, other arithmetic, attend(): weight / jnp.sum(weight, axis=-1, keepdims=True)  30.3 us
    reduce_sum x8, other arithmetic, attend(): jnp.sum(weight, axis=-1, keepdims=True)  28.5 us
    convert_element_type x8, other arithmetic, backward(): d_low = (d_scores * SCALE).astype(LOW)  28 us
  transfers between devices with their start and end apart: 8, of which 4 were waited for; matrix products, arithmetic and copies ran while one was open for 4% of the time, Pallas kernels for 0%

profile of v2, /device:TPU:0, one launch (start us, length us, event | category | flops | bytes accessed | tf_op | source)
XLA Modules:
  0.0 489.1 jit_solution(12119316557051456223)
XLA Ops:
  18.5 47.8 %shard_map.478 = (bf16[4,2,2,2,16,4608]{5,4,3,2,1,0:T(8,128)(2,1)S(1)}, bf16[4,2,2,2,64,512]{5,4,3,2,1,0:T(8,128)(2,1)S(1)}) custom-call(bf16[16,4608]{1,0:T(8,128)(2,1)S(1)} %constant_dynamic-update-slice_fusion.a_one, bf16[64,512]{1,0:T(8,128)(2,1)S(1)} %convert_element_type.299.a_two), custom_call_target="tpu_custom_call" | custom-call | tf_op jit(solution)/shard_map/pallas_call | solution.py:217
  70.1 3.9 fusion.78
  86.2 3.4 broadcast_compare_fusion
  96.4 3.5 fusion.222
  100.6 3.7 broadcast_divide_fusion.4
  104.6 3.5 fusion.221
  108.2 3.7 broadcast_divide_fusion.5
  112.3 3.5 fusion.220
  115.9 3.7 broadcast_divide_fusion.6
  120.1 3.5 fusion.219
  123.6 3.9 broadcast_divide_fusion.7
  134.5 7.2 %fusion.11 = f32[84,3072]{1,0:T(8,128)} fusion(s32[3072]{0:T(1024)} %bitcast.586, s32[3072]{0:T(1024)} %bitcast.590, s32[3072]{0:T(1024)} %bitcast.582, bf16[512,512]{0,1:T(8,128)(2,1)} %fusion.58, f32[1,1,84,3072]{3,1,2,0:T(1,128)} %get-tuple-element.67, f32[]{:T(128)} %bitcast.7, f32[]{:T(128)S(6)} %mul.845, f32[]{:T(128)S(6)} %div.267, ...), kind=kOutput, calls=%fused_computation.23 | convolution fusion | flops 324286464 | bytes 4822024 | tf_op jit(solution)/shard_map/dot_general | solution.py:230
  150.8 4.7 collective-permute-start.3
  171.9 3.8 fusion.226
  175.7 3.7 broadcast_divide_fusion
  179.8 3.5 fusion.225
  183.4 3.7 broadcast_divide_fusion.1
  187.5 3.5 fusion.223
  191.1 3.7 broadcast_divide_fusion.3
  195.2 3.5 fusion.224
  198.8 4.1 broadcast_divide_fusion.2
  209.9 6.1 %multiply_reduce_fusion.8 = (f32[]{:T(128)}, f32[84,3072]{1,0:T(8,128)}) fusion(f32[3072]{0:T(1024)S(1)} %copy-done.184, f32[1,84,3072]{2,0,1:T(1,128)} %param.32, f32[]{:T(128)S(6)} %mul.876, s32[3072]{0:T(1024)S(1)} %bitcast.587, s32[3072]{0:T(1024)S(1)} %bitcast.591, s32[3072]{0:T(1024)S(1)} %bitcast.583, bf16[512,512]{0,1:T(8,128)(2,1)} %fusion.59, ...), kind=kOutput, calls=%fused_computation.191 | convolution fusion | flops 324286464 | bytes 3850252 | tf_op jit(solution)/shard_map/dot_general | solution.py:230
  216.0 3.5 fusion.73
  224.3 4.5 multiply_convert_fusion.1
  228.8 5.2 %fusion.306 = (f32[512]{0:T(512)}, f32[512,512]{1,0:T(8,128)}) fusion(bf16[512,2048]{1,0:T(8,128)(2,1)S(1)} %multiply_convert_fusion.1, bf16[512,4608]{1,0:T(8,128)(2,1)} %bitcast.134), kind=kOutput, calls=%fused_computation.518 | convolution fusion | flops 1074003456 | bytes 5244928 | tf_op jit(solution)/shard_map/dot_general | solution.py:234
  248.3 3.5 multiply_convert_fusion.11
  253.1 3.5 multiply_convert_fusion.10
  258.1 3.5 multiply_convert_fusion.9
  263.0 3.5 multiply_convert_fusion.8
  270.5 4.9 %collective-permute-start.5 = (bf16[64,1024]{0,1:T(8,128)(2,1)S(1)}, bf16[64,1024]{0,1:T(8,128)(2,1)}, u32[]{:S(2)}, u32[]{:S(2)}) collective-permute-start(bf16[64,1024]{0,1:T(8,128)(2,1)S(1)} %get-tuple-element.72), channel_id=1, source_target_pairs={{4,0},{8,4},{12,8},{16,12},{20,16},{24,20},{28,24},{0,28},{5,1},{9... | collective-permute-start | bytes 393224 | tf_op jit(solution)/shard_map/ppermute | solution.py:382
  287.1 4.5 fusion.307
  299.3 4.1 fusion.24
  303.4 3.4 fusion.72
  308.4 3.3 multiply_convert_fusion
  311.7 3.5 fusion.129
  317.8 4.4 fusion.308
  329.8 3.3 fusion.276
  338.7 3.5 multiply_convert_fusion.7
  346.5 5.4 %add_convert_fusion.1 = bf16[2048,512]{1,0:T(8,128)(2,1)S(1)} fusion(f32[2048,512]{1,0:T(8,128)} %fusion.129, f32[512,512]{1,0:T(8,128)} %fusion.230, f32[512,2048]{1,0:T(8,128)} %copy-done.67), kind=kOutput, calls=%fused_computation.12 | convolution fusion | flops 1081344000 | bytes 11534336 | tf_op jit(solution)/shard_map/dot_general | solution.py:238
  354.9 5.1 %add_convert_fusion.2 = bf16[512,2048]{1,0:T(8,128)(2,1)} fusion(f32[512,2048]{1,0:T(8,128)} %fusion.276, bf16[512,2048]{1,0:T(8,128)(2,1)S(1)} %copy-done.80, f32[512,512]{0,1:T(8,128)S(1)} %copy-done.3, f32[512]{0:T(512)S(1)} %bitcast.577, f32[512]{0:T(512)S(1)} %bitcast.570, f32[512]{0:T(512)S(1)} %add_rsqrt_fusion, f32[512]{0:T(512)S(1)} %broadcast_multiply_fusion.8), kind=kOutput, calls=%fused_computation.13 | convolution fusion | flops 1077149696 | bytes 9445376 | tf_op jit(solution)/shard_map/dot_general | solution.py:238
  360.1 3.5 multiply_convert_fusion.6
  365.4 3.5 multiply_convert_fusion.5
  370.8 3.5 multiply_convert_fusion.4
  379.4 4.4 collective-permute-start.7
  385.8 4.2 collective-permute-done.6
  392.8 3.5 fusion.309
  410.7 3.4 fusion.37
  419.3 59.7 %shard_map.479 = (f32[16,4608]{1,0:T(8,128)S(1)}, f32[64,512]{1,0:T(8,128)S(1)}, f32[8,128]{1,0:T(8,128)S(1)}) custom-call(bf16[4,2,2,2,16,4608]{5,4,3,2,1,0:T(8,128)(2,1)} %copy-done.58, bf16[4,2,2,2,64,512]{5,4,3,2,1,0:T(8,128)(2,1)S(1)} %bitcast.150, f32[8,128]{1,0:T(8,128)S(1)} %iota.79.extra), custom_call_target="tpu_custom_call" | custom-call | tf_op jit(solution)/shard_map/pallas_call | solution.py:153
  (643 shorter events, 185.9 us)
Async XLA Ops:
  0.7 13.3 %copy-start.208 = (s32[1,3072]{1,0:T(1,128)S(1)}, s32[1,3072]{1,0:T(1,128)}, u32[]{:S(2)}) copy-start(s32[1,3072]{1,0:T(1,128)} %param.35) | copy-start | bytes 36868
  8.3 61.8 %copy-start.198 = (pred[3072]{0:T(1024)(128)(4,1)}, pred[3072]{0:T(1024)(128)(4,1)S(1)}, u32[]{:S(2)}) copy-start(pred[3072]{0:T(1024)(128)(4,1)S(1)} %get-tuple-element.160) | copy-start | bytes 9220
  10.2 63.8 %copy-start.189 = (f32[512]{0:T(512)}, f32[512]{0:T(512)S(1)}, u32[]{:S(2)}) copy-start(f32[512]{0:T(512)S(1)} %broadcast_maximum_fusion) | copy-start | bytes 6148
  15.5 58.4 %copy-start.119 = (bf16[512,84]{0,1:T(8,128)(2,1)}, bf16[512,84]{0,1:T(8,128)(2,1)S(1)}, u32[]{:S(2)}) copy-start(bf16[512,84]{0,1:T(8,128)(2,1)S(1)} %fusion.75) | copy-start | bytes 258052
  79.7 13.2 %collective-permute-start = (bf16[64,1024]{1,0:T(8,128)(2,1)}, bf16[64,1024]{1,0:T(8,128)(2,1)}, u32[]{:S(2)}, u32[]{:S(2)}) collective-permute-start(bf16[64,1024]{1,0:T(8,128)(2,1)} %get-tuple-element.75), channel_id=1, source_target_pairs={{0,4},{4,8},{8,12},{12,16},{16,20},{20,24},{24,28},{28,0},{1,5},{5... | collective-permute-start | bytes 393224 | tf_op jit(solution)/shard_map/ppermute | solution.py:272
  81.9 11.0 %collective-permute-start.1 = (bf16[64,1024]{1,0:T(8,128)(2,1)}, bf16[64,1024]{1,0:T(8,128)(2,1)}, u32[]{:S(2)}, u32[]{:S(2)}) collective-permute-start(bf16[64,1024]{1,0:T(8,128)(2,1)} %get-tuple-element.76), channel_id=1, source_target_pairs={{4,0},{8,4},{12,8},{16,12},{20,16},{24,20},{28,24},{0,28},{5,1},{9... | collective-permute-start | bytes 393224 | tf_op jit(solution)/shard_map/ppermute | solution.py:273
  94.4 33.2 %copy-start.47 = (bf16[640,1024]{1,0:T(8,128)(2,1)}, bf16[640,1024]{1,0:T(8,128)(2,1)S(1)}, u32[]{:S(2)}) copy-start(bf16[640,1024]{1,0:T(8,128)(2,1)S(1)} %pad_maximum_fusion) | copy-start | bytes 3932164
  95.4 12.8 %copy-start.18 = (f32[512,640]{1,0:T(8,128)}, f32[512,640]{1,0:T(8,128)S(1)}, u32[]{:S(2)}) copy-start(f32[512,640]{1,0:T(8,128)S(1)} %get-tuple-element.116) | copy-start | bytes 3932164
  95.4 12.8 %copy-start.139 = (f32[512]{0:T(512)}, f32[512]{0:T(512)S(1)}, u32[]{:S(2)}) copy-start(f32[512]{0:T(512)S(1)} %get-tuple-element.115) | copy-start | bytes 6148
  95.9 20.0 %copy-start.20 = (f32[512,640]{1,0:T(8,128)}, f32[512,640]{1,0:T(8,128)S(1)}, u32[]{:S(2)}) copy-start(f32[512,640]{1,0:T(8,128)S(1)} %get-tuple-element.118) | copy-start | bytes 3932164
  95.9 20.0 %copy-start.141 = (f32[512]{0:T(512)}, f32[512]{0:T(512)S(1)}, u32[]{:S(2)}) copy-start(f32[512]{0:T(512)S(1)} %get-tuple-element.117) | copy-start | bytes 6148
  96.4 27.2 %copy-start.22 = (f32[512,640]{1,0:T(8,128)}, f32[512,640]{1,0:T(8,128)S(1)}, u32[]{:S(2)}) copy-start(f32[512,640]{1,0:T(8,128)S(1)} %get-tuple-element.112) | copy-start | bytes 3932164
  96.4 27.2 %copy-start.143 = (f32[512]{0:T(512)}, f32[512]{0:T(512)S(1)}, u32[]{:S(2)}) copy-start(f32[512]{0:T(512)S(1)} %get-tuple-element.111) | copy-start | bytes 6148
  104.6 24.4 %copy-start.87 = (bf16[512,128]{0,1:T(8,128)(2,1)}, bf16[512,128]{0,1:T(8,128)(2,1)S(1)}, u32[]{:S(2)}) copy-start(bf16[512,128]{0,1:T(8,128)(2,1)S(1)} %convolution_convert_fusion.18) | copy-start | bytes 393220
  108.2 20.9 %slice-start = ((s8[4718592]{0:T(1024)(128)(4,1)}), s8[4194304]{0:T(1024)(128)(4,1)S(1)}, s32[]{:S(2)}) async-start(s8[4718592]{0:T(1024)(128)(4,1)} %bitcast.142), calls=%async_computation | async-start | bytes 8388608
  112.3 16.7 %copy-start.89 = (bf16[512,128]{0,1:T(8,128)(2,1)}, bf16[512,128]{0,1:T(8,128)(2,1)S(1)}, u32[]{:S(2)}) copy-start(bf16[512,128]{0,1:T(8,128)(2,1)S(1)} %convolution_convert_fusion.19) | copy-start | bytes 393220
  115.9 13.2 %slice-start.1 = ((s8[4718592]{0:T(1024)(128)(4,1)}), s8[524288]{0:T(1024)(128)(4,1)S(1)}, s32[]{:S(2)}) async-start(s8[4718592]{0:T(1024)(128)(4,1)} %bitcast.142), calls=%async_computation.1 | async-start | bytes 1048576
  150.8 16.9 %collective-permute-start.2 = (bf16[64,1024]{1,0:T(8,128)(2,1)}, bf16[64,1024]{1,0:T(8,128)(2,1)}, u32[]{:S(2)}, u32[]{:S(2)}) collective-permute-start(bf16[64,1024]{1,0:T(8,128)(2,1)} %get-tuple-element.73), channel_id=1, source_target_pairs={{0,4},{4,8},{8,12},{12,16},{16,20},{20,24},{24,28},{28,0},{1,5},{5... | collective-permute-start | bytes 393224 | tf_op jit(solution)/shard_map/ppermute | solution.py:272
  150.8 16.9 %collective-permute-start.3 = (bf16[64,1024]{1,0:T(8,128)(2,1)}, bf16[64,1024]{1,0:T(8,128)(2,1)}, u32[]{:S(2)}, u32[]{:S(2)}) collective-permute-start(bf16[64,1024]{1,0:T(8,128)(2,1)} %get-tuple-element.74), channel_id=1, source_target_pairs={{4,0},{8,4},{12,8},{16,12},{20,16},{24,20},{28,24},{0,28},{5,1},{9... | collective-permute-start | bytes 393224 | tf_op jit(solution)/shard_map/ppermute | solution.py:273
  169.9 33.0 %copy-start.49 = (bf16[640,1024]{1,0:T(8,128)(2,1)}, bf16[640,1024]{1,0:T(8,128)(2,1)S(1)}, u32[]{:S(2)}) copy-start(bf16[640,1024]{1,0:T(8,128)(2,1)S(1)} %pad_maximum_fusion.1) | copy-start | bytes 3932164
  170.9 12.5 %copy-start.34 = (f32[512,640]{1,0:T(8,128)}, f32[512,640]{1,0:T(8,128)S(1)}, u32[]{:S(2)}) copy-start(f32[512,640]{1,0:T(8,128)S(1)} %get-tuple-element.126) | copy-start | bytes 3932164
  170.9 12.5 %copy-start.147 = (f32[512]{0:T(512)}, f32[512]{0:T(512)S(1)}, u32[]{:S(2)}) copy-start(f32[512]{0:T(512)S(1)} %get-tuple-element.125) | copy-start | bytes 6148
  171.4 27.3 %copy-start.36 = (f32[512,640]{1,0:T(8,128)}, f32[512,640]{1,0:T(8,128)S(1)}, u32[]{:S(2)}) copy-start(f32[512,640]{1,0:T(8,128)S(1)} %get-tuple-element.128) | copy-start | bytes 3932164
  171.4 27.4 %copy-start.149 = (f32[512]{0:T(512)}, f32[512]{0:T(512)S(1)}, u32[]{:S(2)}) copy-start(f32[512]{0:T(512)S(1)} %get-tuple-element.127) | copy-start | bytes 6148
  171.9 19.1 %copy-start.38 = (f32[512,640]{1,0:T(8,128)}, f32[512,640]{1,0:T(8,128)S(1)}, u32[]{:S(2)}) copy-start(f32[512,640]{1,0:T(8,128)S(1)} %get-tuple-element.130) | copy-start | bytes 3932164
  171.9 19.2 %copy-start.151 = (f32[512]{0:T(512)}, f32[512]{0:T(512)S(1)}, u32[]{:S(2)}) copy-start(f32[512]{0:T(512)S(1)} %get-tuple-element.129) | copy-start | bytes 6148
  179.8 24.5 %copy-start.95 = (bf16[512,128]{0,1:T(8,128)(2,1)}, bf16[512,128]{0,1:T(8,128)(2,1)S(1)}, u32[]{:S(2)}) copy-start(bf16[512,128]{0,1:T(8,128)(2,1)S(1)} %convolution_convert_fusion.14) | copy-start | bytes 393220
  183.4 21.0 %slice-start.2 = ((s8[4718592]{0:T(1024)(128)(4,1)}), s8[4194304]{0:T(1024)(128)(4,1)S(1)}, s32[]{:S(2)}) async-start(s8[4718592]{0:T(1024)(128)(4,1)} %bitcast.146), calls=%async_computation.2 | async-start | bytes 8388608
  187.5 16.9 %copy-start.97 = (bf16[512,128]{0,1:T(8,128)(2,1)}, bf16[512,128]{0,1:T(8,128)(2,1)S(1)}, u32[]{:S(2)}) copy-start(bf16[512,128]{0,1:T(8,128)(2,1)S(1)} %convolution_convert_fusion.15) | copy-start | bytes 393220
  191.1 13.3 %slice-start.3 = ((s8[4718592]{0:T(1024)(128)(4,1)}), s8[524288]{0:T(1024)(128)(4,1)S(1)}, s32[]{:S(2)}) async-start(s8[4718592]{0:T(1024)(128)(4,1)} %bitcast.146), calls=%async_computation.3 | async-start | bytes 1048576
  269.6 14.2 %copy-start.205 = (s32[1,128]{1,0:T(1,128)S(1)}, s32[1,128]{1,0:T(1,128)}, u32[]{:S(2)}) copy-start(s32[1,128]{1,0:T(1,128)} %param.38) | copy-start | bytes 1540
  270.5 11.2 %collective-permute-start.4 = (bf16[64,1024]{0,1:T(8,128)(2,1)}, bf16[64,1024]{0,1:T(8,128)(2,1)}, u32[]{:S(2)}, u32[]{:S(2)}) collective-permute-start(bf16[64,1024]{0,1:T(8,128)(2,1)} %get-tuple-element.71), channel_id=1, source_target_pairs={{0,4},{4,8},{8,12},{12,16},{16,20},{20,24},{24,28},{28,0},{1,5},{5... | collective-permute-start | bytes 393224 | tf_op jit(solution)/shard_map/ppermute | solution.py:383
  270.5 13.3 %collective-permute-start.5 = (bf16[64,1024]{0,1:T(8,128)(2,1)S(1)}, bf16[64,1024]{0,1:T(8,128)(2,1)}, u32[]{:S(2)}, u32[]{:S(2)}) collective-permute-start(bf16[64,1024]{0,1:T(8,128)(2,1)S(1)} %get-tuple-element.72), channel_id=1, source_target_pairs={{4,0},{8,4},{12,8},{16,12},{20,16},{24,20},{28,24},{0,28},{5,1},{9... | collective-permute-start | bytes 393224 | tf_op jit(solution)/shard_map/ppermute | solution.py:382
  327.6 9.8 %copy-start.63 = (bf16[512,512]{1,0:T(8,128)(2,1)}, bf16[512,512]{1,0:T(8,128)(2,1)S(1)}, u32[]{:S(2)}) copy-start(bf16[512,512]{1,0:T(8,128)(2,1)S(1)} %convolution_convert_fusion.2) | copy-start | bytes 1572868
  354.9 10.1 %copy-start.71 = (bf16[512,1536]{1,0:T(8,128)(2,1)S(1)}, bf16[512,1536]{1,0:T(8,128)(2,1)}, u32[]{:S(2)}) copy-start(bf16[512,1536]{1,0:T(8,128)(2,1)} %copy-done.68) | copy-start | bytes 4718596
  378.7 13.6 %copy-start.206 = (s32[1,128]{1,0:T(1,128)S(1)}, s32[1,128]{1,0:T(1,128)}, u32[]{:S(2)}) copy-start(s32[1,128]{1,0:T(1,128)} %param.38) | copy-start | bytes 1540
  378.9 11.1 %collective-permute-start.6 = (bf16[64,1024]{0,1:T(8,128)(2,1)S(1)}, bf16[64,1024]{0,1:T(8,128)(2,1)S(1)}, u32[]{:S(2)}, u32[]{:S(2)}) collective-permute-start(bf16[64,1024]{0,1:T(8,128)(2,1)S(1)} %get-tuple-element.69), channel_id=1, source_target_pairs={{0,4},{4,8},{8,12},{12,16},{16,20},{20,24},{24,28},{28,0},{1,5},{5... | collective-permute-start | bytes 393224 | tf_op jit(solution)/shard_map/ppermute | solution.py:383
  379.4 12.8 %collective-permute-start.7 = (bf16[64,1024]{0,1:T(8,128)(2,1)S(1)}, bf16[64,1024]{0,1:T(8,128)(2,1)S(1)}, u32[]{:S(2)}, u32[]{:S(2)}) collective-permute-start(bf16[64,1024]{0,1:T(8,128)(2,1)S(1)} %get-tuple-element.70), channel_id=1, source_target_pairs={{4,0},{8,4},{12,8},{16,12},{20,16},{24,20},{28,24},{0,28},{5,1},{9... | collective-permute-start | bytes 393224 | tf_op jit(solution)/shard_map/ppermute | solution.py:382
  419.2 61.2 %copy-start.135 = (f32[16,84]{1,0:T(8,128)S(1)}, f32[16,84]{1,0:T(8,128)}, u32[]{:S(2)}) copy-start(f32[16,84]{1,0:T(8,128)} %param.47) | copy-start | bytes 16132
  419.2 62.6 %copy-start.125 = (f32[168,16]{0,1:T(8,128)S(1)}, f32[168,16]{0,1:T(8,128)}, u32[]{:S(2)}) copy-start(f32[168,16]{0,1:T(8,128)} %param.41) | copy-start | bytes 32260
  419.2 62.6 %copy-start.175 = (f32[168,16]{0,1:T(8,128)S(1)}, f32[168,16]{0,1:T(8,128)}, u32[]{:S(2)}) copy-start(f32[168,16]{0,1:T(8,128)} %param.48) | copy-start | bytes 32260
  419.2 63.9 %copy-start.116 = (f32[16,512]{1,0:T(8,128)S(1)}, f32[16,512]{1,0:T(8,128)}, u32[]{:S(2)}) copy-start(f32[16,512]{1,0:T(8,128)} %param.43) | copy-start | bytes 98308
  419.2 63.9 %copy-start.133 = (f32[16,512]{1,0:T(8,128)S(1)}, f32[16,512]{1,0:T(8,128)}, u32[]{:S(2)}) copy-start(f32[16,512]{1,0:T(8,128)} %param.50) | copy-start | bytes 98308
  419.2 63.9 %copy-start.134 = (f32[16,512]{1,0:T(8,128)S(1)}, f32[16,512]{1,0:T(8,128)}, u32[]{:S(2)}) copy-start(f32[16,512]{1,0:T(8,128)} %param.57) | copy-start | bytes 98308
  419.2 64.6 %copy-start.108 = (f32[16,1536]{1,0:T(8,128)S(1)}, f32[16,1536]{1,0:T(8,128)}, u32[]{:S(2)}) copy-start(f32[16,1536]{1,0:T(8,128)} %param.42) | copy-start | bytes 294916
  419.2 66.2 %copy-start.103 = (f32[16,2048]{1,0:T(8,128)S(1)}, f32[16,2048]{1,0:T(8,128)}, u32[]{:S(2)}) copy-start(f32[16,2048]{1,0:T(8,128)} %param.44) | copy-start | bytes 393220
  419.3 66.2 %copy-start.111 = (f32[16,2048]{1,0:T(8,128)S(1)}, f32[16,2048]{1,0:T(8,128)}, u32[]{:S(2)}) copy-start(f32[16,2048]{1,0:T(8,128)} %param.51) | copy-start | bytes 393220
  419.3 66.2 %copy-start.112 = (f32[16,2048]{1,0:T(8,128)S(1)}, f32[16,2048]{1,0:T(8,128)}, u32[]{:S(2)}) copy-start(f32[16,2048]{1,0:T(8,128)} %param.58) | copy-start | bytes 393220
  (178 other events, 567.2 us)
